TPU v7x, 32 devices: a whole 2x2x4 slice. The times are simulated.
32 devices in a mesh: dp: 4 (over y, x), fsdp: 8 (over z, core).
Axes of the slice: x: 2, y: 2, z: 4, core: 2. Of those that a mesh axis runs over, the one named last changes fastest.
Arguments:
- tokens: bfloat16 [32768, 768], P(('dp', 'fsdp')), may hold values from -6 to 6
- cotangent: bfloat16 [32768, 768], P(('dp', 'fsdp')), may hold values from -6 to 6
- image_ids: int32 [32768], P(('dp', 'fsdp')), may hold values from -1 to 4, as said below
- patch_grid: int32 [2, 32768], P(None, ('dp', 'fsdp')), may hold values from 0 to 23, as said below
- qkv_weight: float32 [768, 2304], P('fsdp')
- out_weight: float32 [768, 768], P('fsdp')
- up_weight: float32 [768, 3072], P('fsdp')
- down_weight: float32 [3072, 768], P('fsdp')
- vectors: float32 [10752], P('fsdp')
- qkv_first: float32 [768, 2304], P('fsdp'), may hold values from -80 to 80
- out_first: float32 [768, 768], P('fsdp'), may hold values from -12 to 12
- up_first: float32 [768, 3072], P('fsdp'), may hold values from -40 to 40
- down_first: float32 [3072, 768], P('fsdp'), may hold values from -64 to 64
- vector_first: float32 [10752], P('fsdp'), may hold values from -64 to 64
- qkv_second: float32 [768, 2304], P('fsdp')
- out_second: float32 [768, 768], P('fsdp')
- up_second: float32 [768, 3072], P('fsdp')
- down_second: float32 [3072, 768], P('fsdp')
- vector_second: float32 [10752], P('fsdp'), may hold values from 11.79648 to 47.18592
Outputs:
- output: bfloat16 [32768, 768], P(('dp', 'fsdp'))
- tokens_grad: bfloat16 [32768, 768], P(('dp', 'fsdp'))
- qkv_grad: float32 [768, 2304], P('fsdp')
- out_grad: float32 [768, 768], P('fsdp')
- up_grad: float32 [768, 3072], P('fsdp')
- down_grad: float32 [3072, 768], P('fsdp')
- vector_grad: float32 [10752], P('fsdp')
- down_bias_grad: float32 [768], replicated
- qkv_first_new: float32 [768, 2304], P('fsdp')
- out_first_new: float32 [768, 768], P('fsdp')
- up_first_new: float32 [768, 3072], P('fsdp')
- down_first_new: float32 [3072, 768], P('fsdp')
- vector_first_new: float32 [10752], P('fsdp')
- qkv_second_new: float32 [768, 2304], P('fsdp')
- out_second_new: float32 [768, 768], P('fsdp')
- up_second_new: float32 [768, 3072], P('fsdp')
- down_second_new: float32 [3072, 768], P('fsdp')
- vector_second_new: float32 [10752], P('fsdp')
- qkv_weight_new: float32 [768, 2304], P('fsdp')
- out_weight_new: float32 [768, 768], P('fsdp')
- up_weight_new: float32 [768, 3072], P('fsdp')
- down_weight_new: float32 [3072, 768], P('fsdp')
- vectors_new: float32 [10752], P('fsdp')
- weight_norms: float32 [4], replicated
- update_norms: float32 [4], replicated
Inputs may be any that keep to these rules, and one draw needn't show every extreme that they name: `image_ids`: each device's 1024 slots form one unit of 1024 slots. A unit holds whole images in a row from its first slot, one of four sets that is the same in all units of a device: five of 14 x 14 patches; two of 20 x 20 and one of 14 x 14; one of 24 x 24 and one of 20 x 20; one of 24 x 24 and two of 14 x 14. Image k of unit u has id 5u + k; the rest of every unit is padding with id -1. `patch_grid`: row 0 holds each patch's row and row 1 its column in its image's square grid, patches in row-major order; padding has 0 in both.
All inputs are finite; a program needn't handle non-finite values.
Results may differ from a plain program's by a relative error of at most 0.013.
The roundings to bfloat16 on the way count: a program that leaves them out, or rounds other values in their place, can miss the bound.
Values may be sent and summed in bfloat16 or wider, within the bound.
No kernel may reach another device: no remote copies, remote signals or barrier semaphores. Data moves between devices by JAX's collectives and lax.ppermute only.
A program may use at most 192 MiB of HBM per device.

v0:
```python
from functools import partial

import jax
import jax.numpy as jnp
from jax import lax
from jax.sharding import PartitionSpec as P

H = 12
HD = 64
STEP = 10


norm_eps = 1e-06
masked_fill = -1e30


def layer_norm(values, norm_gain, norm_shift):
    centre = jnp.mean(values, axis=-1, keepdims=True)
    centred = values - centre
    spread = jnp.mean(centred * centred, axis=-1, keepdims=True)
    return centred * lax.rsqrt(spread + norm_eps) * norm_gain + norm_shift


def rotate(head_rows, angles):
    half = head_rows.shape[-1] // 2
    lower_half = head_rows[..., :half]
    upper_half = head_rows[..., half:]
    cosine = jnp.cos(angles)
    sine_part = jnp.sin(angles)
    return jnp.concatenate(
        [
            lower_half * cosine - upper_half * sine_part,
            lower_half * sine_part + upper_half * cosine,
        ],
        axis=-1,
    )


def split_vector(packed, width, hidden_width):
    lengths = [width, width, width, width, 3 * width, width, hidden_width, width, width]
    pieces = []
    offset = 0
    for length in lengths:
        pieces.append(packed[offset : offset + length])
        offset += length
    return pieces


def exact_gelu(values):
    return jax.nn.gelu(values, approximate=False)


def across_rows(left, right):
    return lax.dot_general(
        left, right, (((0,), (0,)), ((), ())), preferred_element_type=jnp.float32
    )


def against_columns(left, right):
    return lax.dot_general(
        left, right, (((1,), (1,)), ((), ())), preferred_element_type=jnp.float32
    )


def attend_forward(inputs, same_image, scale):
    query, key_rows, value_rows = inputs
    scores = against_columns(query, key_rows) * scale
    masked = jnp.where(same_image, scores, masked_fill)
    peak = jnp.max(masked, axis=1, keepdims=True)
    weights = jnp.exp(masked - peak)
    total = jnp.sum(weights, axis=1, keepdims=True)
    probs = (weights / total).astype(jnp.bfloat16)
    mixed = jnp.dot(probs, value_rows, preferred_element_type=jnp.float32).astype(jnp.bfloat16)
    return (mixed, (peak + jnp.log(total))[:, 0])


def attend_backward(inputs, same_image, scale):
    query, key_rows, value_rows, grad_mixed, log_total = inputs
    scores = against_columns(query, key_rows) * scale
    masked = jnp.where(same_image, scores, masked_fill)
    probs = jnp.exp(masked - log_total[:, None])
    grad_probs = against_columns(grad_mixed, value_rows)
    delta = jnp.sum(probs * grad_probs, axis=1, keepdims=True)
    grad_scores = jnp.where(same_image, probs * (grad_probs - delta), 0.0).astype(jnp.bfloat16)
    grad_query = jnp.dot(grad_scores, key_rows, preferred_element_type=jnp.float32) * scale
    grad_key = across_rows(grad_scores, query) * scale
    grad_value = across_rows(probs.astype(jnp.bfloat16), grad_mixed)
    return (grad_query, grad_key, grad_value)


def adam_terms(grad, first, second, master, decay):
    first_new = 0.9 * first + 0.1 * grad
    second_new = 0.999 * second + 0.001 * grad * grad
    first_hat = first_new / (1.0 - 0.9**STEP)
    second_hat = second_new / (1.0 - 0.999**STEP)
    update = first_hat / (jnp.sqrt(second_hat) + 1e-06) + decay * master
    return (first_new, second_new, update)


def body(
    tokens,
    cotangent,
    image_ids,
    patch_grid,
    qkv_weight,
    out_weight,
    up_weight,
    down_weight,
    vectors,
    qkv_first,
    out_first,
    up_first,
    down_first,
    vector_first,
    qkv_second,
    out_second,
    up_second,
    down_second,
    vector_second,
):
    rows = tokens.shape[0]
    width = tokens.shape[1]
    hidden_width = up_weight.shape[1]
    scale = HD ** (-0.5)
    masters = (qkv_weight, out_weight, up_weight, down_weight)
    low_qkv = qkv_weight.astype(jnp.bfloat16)
    low_out = out_weight.astype(jnp.bfloat16)
    low_up = up_weight.astype(jnp.bfloat16)
    low_down = down_weight.astype(jnp.bfloat16)
    low_vectors = vectors.astype(jnp.bfloat16)
    full_qkv, full_out, full_up, full_down, full_vectors = (
        lax.all_gather(low_qkv, "fsdp", axis=0, tiled=True),
        lax.all_gather(low_out, "fsdp", axis=0, tiled=True),
        lax.all_gather(low_up, "fsdp", axis=0, tiled=True),
        lax.all_gather(low_down, "fsdp", axis=0, tiled=True),
        lax.all_gather(low_vectors, "fsdp", axis=0, tiled=True),
    )
    gain_one, shift_one, gain_two, shift_two, bias_qkv, bias_out, bias_up, bias_down, freq_flat = (
        split_vector(full_vectors.astype(jnp.float32), width, hidden_width)
    )
    freqs = freq_flat.reshape(2, H, HD // 2)
    given = cotangent.astype(jnp.float32) * (image_ids >= 0).astype(jnp.float32)[:, None]
    grid_rows = patch_grid[0].astype(jnp.float32)
    grid_cols = patch_grid[1].astype(jnp.float32)

    def rotary(query_part, key_part, freq_table):
        angles = (
            grid_rows[:, None, None] * freq_table[0][None]
            + grid_cols[:, None, None] * freq_table[1][None]
        )
        return (rotate(query_part, angles), rotate(key_part, angles))

    inputs = tokens.astype(jnp.float32)
    normed_one = layer_norm(inputs, gain_one, shift_one).astype(jnp.bfloat16)
    projected = jnp.dot(normed_one, full_qkv, preferred_element_type=jnp.float32) + bias_qkv
    queries = projected[:, :width].reshape(rows, H, HD)
    keys = projected[:, width : 2 * width].reshape(rows, H, HD)
    values = projected[:, 2 * width :].reshape(rows, H, HD).astype(jnp.bfloat16)
    queries_rot, keys_rot = rotary(queries, keys, freqs)
    query_heads = queries_rot.astype(jnp.bfloat16).transpose(1, 0, 2)
    key_heads = keys_rot.astype(jnp.bfloat16).transpose(1, 0, 2)
    value_heads = values.transpose(1, 0, 2)
    same_image = image_ids[:, None] == image_ids[None, :]
    mixed_heads, log_total = lax.map(
        partial(attend_forward, same_image=same_image, scale=scale),
        (query_heads, key_heads, value_heads),
    )
    mixed = mixed_heads.transpose(1, 0, 2).reshape(rows, width)
    resid = inputs + jnp.dot(mixed, full_out, preferred_element_type=jnp.float32) + bias_out
    normed_two = layer_norm(resid, gain_two, shift_two).astype(jnp.bfloat16)
    hidden = jnp.dot(normed_two, full_up, preferred_element_type=jnp.float32) + bias_up
    active = exact_gelu(hidden).astype(jnp.bfloat16)
    output = (
        resid + jnp.dot(active, full_down, preferred_element_type=jnp.float32) + bias_down
    ).astype(jnp.bfloat16)
    back_qkv, back_out, back_up, back_down = (
        lax.all_gather(low_qkv, "fsdp", axis=0, tiled=True),
        lax.all_gather(low_out, "fsdp", axis=0, tiled=True),
        lax.all_gather(low_up, "fsdp", axis=0, tiled=True),
        lax.all_gather(low_down, "fsdp", axis=0, tiled=True),
    )
    given_low = given.astype(jnp.bfloat16)
    down_grad = across_rows(active, given_low)
    grad_bias_down = jnp.sum(given, axis=0)
    down_bias_grad = lax.psum(grad_bias_down, ("dp", "fsdp"))
    grad_active = against_columns(given_low, back_down)
    unused_gelu, gelu_pull = jax.vjp(exact_gelu, hidden)
    grad_hidden = gelu_pull(grad_active)[0].astype(jnp.bfloat16)
    up_grad = across_rows(normed_two, grad_hidden)
    grad_bias_up = jnp.sum(grad_hidden.astype(jnp.float32), axis=0)
    grad_normed_two = against_columns(grad_hidden, back_up)
    unused_two, norm_pull_two = jax.vjp(layer_norm, resid, gain_two, shift_two)
    grad_resid_part, grad_gain_two, grad_shift_two = norm_pull_two(grad_normed_two)
    grad_resid = given + grad_resid_part
    grad_branch = grad_resid.astype(jnp.bfloat16)
    out_grad = across_rows(mixed, grad_branch)
    grad_bias_out = jnp.sum(grad_branch.astype(jnp.float32), axis=0)
    grad_mixed = against_columns(grad_branch, back_out).astype(jnp.bfloat16)
    grad_mixed_heads = grad_mixed.reshape(rows, H, HD).transpose(1, 0, 2)
    grad_query_heads, grad_key_heads, grad_value_heads = lax.map(
        partial(attend_backward, same_image=same_image, scale=scale),
        (query_heads, key_heads, value_heads, grad_mixed_heads, log_total),
    )
    unused_rot, rotary_pull = jax.vjp(rotary, queries, keys, freqs)
    grad_queries, grad_keys, grad_freqs = rotary_pull(
        (grad_query_heads.transpose(1, 0, 2), grad_key_heads.transpose(1, 0, 2))
    )
    grad_values = grad_value_heads.transpose(1, 0, 2)
    grad_projected = jnp.concatenate(
        [
            grad_queries.reshape(rows, width),
            grad_keys.reshape(rows, width),
            grad_values.reshape(rows, width),
        ],
        axis=1,
    ).astype(jnp.bfloat16)
    qkv_grad = across_rows(normed_one, grad_projected)
    grad_bias_qkv = jnp.sum(grad_projected.astype(jnp.float32), axis=0)
    grad_normed_one = against_columns(grad_projected, back_qkv)
    unused_one, norm_pull_one = jax.vjp(layer_norm, inputs, gain_one, shift_one)
    grad_tokens_part, grad_gain_one, grad_shift_one = norm_pull_one(grad_normed_one)
    tokens_grad = (grad_resid + grad_tokens_part).astype(jnp.bfloat16)
    vector_grad = jnp.concatenate(
        [
            grad_gain_one,
            grad_shift_one,
            grad_gain_two,
            grad_shift_two,
            grad_bias_qkv,
            grad_bias_out,
            grad_bias_up,
            grad_bias_down,
            grad_freqs.reshape(-1),
        ]
    )
    group_grads = (
        lax.psum_scatter(qkv_grad, "fsdp", scatter_dimension=0, tiled=True),
        lax.psum_scatter(out_grad, "fsdp", scatter_dimension=0, tiled=True),
        lax.psum_scatter(up_grad, "fsdp", scatter_dimension=0, tiled=True),
        lax.psum_scatter(down_grad, "fsdp", scatter_dimension=0, tiled=True),
        lax.psum_scatter(vector_grad, "fsdp", scatter_dimension=0, tiled=True),
    )
    reduced = lax.psum(
        (group_grads[0], group_grads[1], group_grads[2], group_grads[3], group_grads[4]), "dp"
    )
    firsts = (qkv_first, out_first, up_first, down_first)
    seconds = (qkv_second, out_second, up_second, down_second)
    first_list = []
    second_list = []
    update_list = []
    for index in range(4):
        first_new, second_new, update = adam_terms(
            reduced[index], firsts[index], seconds[index], masters[index], 0.01
        )
        first_list.append(first_new)
        second_list.append(second_new)
        update_list.append(update)
    update_local = jnp.stack([jnp.sum(update * update) for update in update_list])
    weight_local = jnp.stack([jnp.sum(matrix * matrix) for matrix in masters])
    weight_squares, update_squares = lax.psum((weight_local, update_local), "fsdp")
    weight_norms = jnp.sqrt(weight_squares)
    update_norms = jnp.sqrt(update_squares)
    new_list = []
    for index in range(4):
        ratio = weight_norms[index] / (update_norms[index] + 1e-06)
        new_list.append(masters[index] - 0.3 * ratio * update_list[index])
    vector_first_new, vector_second_new, vector_update = adam_terms(
        reduced[4], vector_first, vector_second, vectors, 0.0
    )
    vectors_new = vectors - 0.2 * vector_update
    return (
        output,
        tokens_grad,
        reduced[0],
        reduced[1],
        reduced[2],
        reduced[3],
        reduced[4],
        down_bias_grad,
        first_list[0],
        first_list[1],
        first_list[2],
        first_list[3],
        vector_first_new,
        second_list[0],
        second_list[1],
        second_list[2],
        second_list[3],
        vector_second_new,
        new_list[0],
        new_list[1],
        new_list[2],
        new_list[3],
        vectors_new,
        weight_norms,
        update_norms,
    )


def solution(mesh):
    in_specs = (
        P(("dp", "fsdp"), None),
        P(("dp", "fsdp"), None),
        P(("dp", "fsdp")),
        P(None, ("dp", "fsdp")),
        P("fsdp", None),
        P("fsdp", None),
        P("fsdp", None),
        P("fsdp", None),
        P("fsdp"),
        P("fsdp", None),
        P("fsdp", None),
        P("fsdp", None),
        P("fsdp", None),
        P("fsdp"),
        P("fsdp", None),
        P("fsdp", None),
        P("fsdp", None),
        P("fsdp", None),
        P("fsdp"),
    )
    out_specs = (
        P(("dp", "fsdp"), None),
        P(("dp", "fsdp"), None),
        P("fsdp", None),
        P("fsdp", None),
        P("fsdp", None),
        P("fsdp", None),
        P("fsdp"),
        P(),
        P("fsdp", None),
        P("fsdp", None),
        P("fsdp", None),
        P("fsdp", None),
        P("fsdp"),
        P("fsdp", None),
        P("fsdp", None),
        P("fsdp", None),
        P("fsdp", None),
        P("fsdp"),
        P("fsdp", None),
        P("fsdp", None),
        P("fsdp", None),
        P("fsdp", None),
        P("fsdp"),
        P(),
        P(),
    )
    return jax.shard_map(body, mesh=mesh, in_specs=in_specs, out_specs=out_specs, check_vma=False)
```

profile of v0, /device:TPU:0, one launch (start us, length us, event | category | flops | bytes accessed | tf_op | source)
XLA Modules:
  0.0 932.3 jit_solution(3916346632022710716)
XLA Ops:
  14.7 31.5 %all-reduce.6 = bf16[10752]{0:T(1024)(128)(2,1)S(1)} all-reduce(bf16[10752]{0:T(1024)(128)(2,1)S(1)} %dynamic-update-slice), channel_id=1, replica_groups=mesh['dp'=4,'fsdp'=8] {'fsdp'}, use_global_device_ids=true, to_apply=%add.6 | all-reduce | flops 10752 | bytes 43008
  51.9 3.2 all-gather.5.cloned.1.call-done
  55.1 6.3 convolution_add_fusion
  61.4 3.1 fusion.104
  64.6 3.5 copy.83
  68.2 3.6 copy.84
  71.8 10.8 %subtract_convert_fusion = (bf16[1024,12,32]{0,2,1:T(8,128)(2,1)S(1)}, bf16[1024,12,32]{0,2,1:T(8,128)(2,1)S(1)}, bf16[1024,12,32]{0,2,1:T(8,128)(2,1)S(1)}, bf16[1024,12,32]{0,2,1:T(8,128)(2,1)S(1)}) fusion(f32[1024,12,64]{0,2,1:T(8,128)} %bitcast.148, f32[12,32]{1,0:T(8,128)S(1)} %slice.127, f32[1024]{0:T(1024)S(1)} %bitcast.167, ...), kind=kLoop, calls=%fused_computation.126 | loop fusion | flops 7471104 | bytes 9448448 | tf_op jit(solution)/shard_map/convert.8
  84.8 4.2 copy.86
  89.0 4.2 copy.87
  94.8 4.1 copy.88
  98.9 110.6 %while.28 = (s32[]{:T(128)}, bf16[12,1024,64]{1,2,0:T(8,128)(2,1)}, f32[12,1024]{1,0:T(8,128)S(1)}, bf16[12,1024,64]{2,1,0:T(8,128)(2,1)}, bf16[12,1024,64]{2,1,...) while((s32[]{:T(128)}, bf16[12,1024,64]{1,2,0:T(8,128)(2,1)}, ...), condition=%wide.region_5.6_spmd.clone, body=%wide.region_2.5_spmd.clone.sunk | while | flops 284228608 | bytes 30341244 | solution.py:164
  104.0 4.2 fusion.152
  113.2 4.2 fusion.152
  122.4 4.2 fusion.152
  131.5 4.2 fusion.152
  140.7 4.6 fusion.152
  150.2 4.2 fusion.152
  159.4 4.3 fusion.152
  168.6 4.3 fusion.152
  177.8 4.2 fusion.152
  187.0 4.2 fusion.152
  196.1 4.2 fusion.152
  205.2 4.2 fusion.152
  209.4 3.4 fusion.110
  214.9 37.8 %multiply_convert_fusion = (bf16[1024,3072]{1,0:T(8,128)(2,1)}, f32[1024,3072]{1,0:T(8,128)}, f32[1024,3072]{1,0:T(8,128)}) fusion(f32[3072]{0:T(1024)S(1)} %slice.161, bf16[768,3072]{1,0:T(8,128)(2,1)} %all-gather.9.cloned.1.call-done, f32[1024,768]{0,1:T(8,128)} %copy-done.5, f32[768]{0:T(1024)S(1)} %get-tuple-element.380, ...), kind=kOutput, calls=%fused_computation.64 | convolution fusion | flops 5043388416 | bytes 39348224 | tf_op jit(solution)/shard_map/dot_general | solution.py:171
  252.8 18.1 %convert_reduce_fusion = (f32[3072]{0:T(1024)}, bf16[1024,3072]{1,0:T(8,128)(2,1)}) fusion(f32[1024,3072]{1,0:T(8,128)} %get-tuple-element.359, bf16[3072,768]{1,0:T(8,128)(2,1)} %all-gather.11.cloned.1.call-done, bf16[1024,768]{0,1:T(8,128)(2,1)S(1)} %copy-done.11, f32[1024]{0:T(1024)S(1)} %copy-done.64, f32[1024,3072]{1,0:T(8,128)} %get-tuple-element.401, ...), kind=kOutput, calls=%fused_computation.62 | convolution fusion | flops 4887671808 | bytes 37777408 | tf_op jit(solution)/shard_map/dot_general | solution.py:60
  270.8 10.4 %fusion.112 = (f32[768]{0:T(1024)}, f32[1024,768]{1,0:T(8,128)}) fusion(bf16[1024,3072]{1,0:T(8,128)(2,1)} %get-tuple-element.407, bf16[768,3072]{1,0:T(8,128)(2,1)} %all-gather.9.cloned.1.call-done), kind=kOutput, calls=%fused_computation.202 | convolution fusion | flops 4832623616 | bytes 14158848 | tf_op jit(solution)/shard_map/dot_general | solution.py:60
  281.2 3.7 copy.91
  285.0 3.5 multiply_reduce_fusion.1
  300.4 144.7 %while.29 = (s32[]{:T(128)}, f32[12,1024,64]{1,2,0:T(8,128)}, f32[12,1024,64]{1,2,0:T(8,128)}, bf16[12,1024,64]{1,2,0:T(8,128)(2,1)}, bf16[12,1024,64]{2,1,0:T(8...) while((s32[]{:T(128)}, f32[12,1024,64]{1,2,0:T(8,128)}, ...), condition=%wide.region_12.13_spmd.clone, body=%wide.region_10.12_spmd.clone.sunk | while | flops 683801600 | bytes 34116720 | solution.py:200
  445.2 12.0 %multiply_add_fusion = (f32[1024,12,32]{0,2,1:T(8,128)S(1)}, f32[1024,12,32]{0,2,1:T(8,128)S(1)}, f32[1024,12,32]{0,2,1:T(8,128)S(1)}, f32[1024,12,32]{0,2,1:T(8,128)S(1)}) fusion(f32[1024,12,64]{0,2,1:T(8,128)} %bitcast.150, f32[1024,12,64]{0,2,1:T(8,128)} %bitcast.160, f32[1024,12,64]{0,2,1:T(8,128)} %bitcast.149, f32[1024,12,64]{0,2,1:T(8,128)S(1)} %bitcast.147, ...), kind=kLoop, calls=%fused_computation.120 | loop fusion | flops 13762560 | bytes 18885632 | tf_op jit(solution)/shard_map/transpose(jvp())/add_any | solution.py:28
  459.7 6.1 multiply_reduce_fusion.5
  467.6 8.4 fusion.90
  476.1 10.5 %fusion.94 = f32[768,3072]{1,0:T(8,128)} fusion(bf16[1024,3072]{1,0:T(8,128)(2,1)} %get-tuple-element.407, f32[1024,768]{0,1:T(8,128)} %copy-done.5, f32[768]{0:T(1024)S(1)} %get-tuple-element.380, f32[768]{0:T(1024)S(1)} %get-tuple-element.379, f32[1024]{0:T(1024)S(1)} %fusion.89, f32[1024]{0:T(1024)S(1)} %broadcast_multiply_fusion), kind=kOutput, calls=%fused_computation.191 | convolution fusion | flops 4835770368 | bytes 18888704 | tf_op jit(solution)/shard_map/dot_general | solution.py:54
  488.0 10.2 %fusion.79 = f32[3072,768]{1,0:T(8,128)} fusion(bf16[1024,3072]{1,0:T(8,128)(2,1)} %get-tuple-element.358, bf16[1024,768]{0,1:T(8,128)(2,1)S(1)} %copy-done.13, f32[1024]{0:T(1024)S(1)} %copy-done.64), kind=kOutput, calls=%fused_computation.132 | convolution fusion | flops 4834197504 | bytes 17305600 | tf_op jit(solution)/shard_map/dot_general | solution.py:54
  498.9 9.7 %fusion.111 = (f32[768]{0:T(1024)}, f32[1024,768]{1,0:T(8,128)}) fusion(bf16[768,2304]{1,0:T(8,128)(2,1)} %all-gather.5.cloned.1.call-done, bf16[1024,768]{0,1:T(8,128)(2,1)} %bitcast.19, bf16[1024,768]{0,1:T(8,128)(2,1)} %bitcast.158, bf16[1024,768]{0,1:T(8,128)(2,1)} %bitcast.155), kind=kOutput, calls=%fused_computation.201 | convolution fusion | flops 3638820096 | bytes 11406336 | tf_op jit(solution)/shard_map/dot_general | solution.py:60
  508.6 3.9 copy.96
  520.1 31.9 %reduce-scatter.5.cloned.1.call-done = f32[96,2304]{1,0:T(8,128)} async-done(((f32[768,2304]{1,0:T(8,128)}), f32[96,2304]{1,0:T(8,128)}) %reduce-scatter.5.cloned.1.call-update) | async-done | bytes 884752 | tf_op jit(solution)/shard_map/reduce_scatter | solution.py:237
  552.0 100.2 %reduce-scatter.9.cloned.1.call-done = f32[96,3072]{1,0:T(8,128)} async-done(((f32[768,3072]{1,0:T(8,128)}), f32[96,3072]{1,0:T(8,128)}) %reduce-scatter.9.cloned.1.call-update) | async-done | bytes 1179664 | tf_op jit(solution)/shard_map/reduce_scatter | solution.py:239
  652.2 100.2 %reduce-scatter.11.cloned.1.call-done = f32[384,768]{1,0:T(8,128)} async-done(((f32[3072,768]{1,0:T(8,128)}), f32[384,768]{1,0:T(8,128)}) %reduce-scatter.11.cloned.1.call-update) | async-done | bytes 1179664 | tf_op jit(solution)/shard_map/reduce_scatter | solution.py:240
  755.3 9.6 %add_convert_fusion.4 = bf16[1024,768]{0,1:T(8,128)(2,1)} fusion(f32[1024,768]{0,1:T(8,128)S(1)} %copy-done.7, bf16[1024,3072]{1,0:T(8,128)(2,1)} %get-tuple-element.358, bf16[3072,768]{1,0:T(8,128)(2,1)} %all-gather.11.cloned.1.call-done, f32[768]{0:T(1024)S(1)} %copy-done.75), kind=kOutput, calls=%fused_computation.109 | convolution fusion | flops 4834197504 | bytes 15731712 | tf_op jit(solution)/shard_map/dot_general | solution.py:174
  767.5 38.1 %psum.61 = f32[768]{0:T(1024)} all-reduce(f32[768]{0:T(1024)S(1)} %get-tuple-element.374), channel_id=1, replica_groups=mesh['dp'=4,'fsdp'=8] {'dp','fsdp'}, use_global_device_ids=true, to_apply=%region_35.36 | all-reduce | flops 768 | bytes 6144 | tf_op jit(solution)/shard_map/psum | solution.py:185
  808.6 40.9 %all-reduce.12.cloned.1.call-done = (f32[96,2304]{1,0:T(8,128)}, f32[96,768]{1,0:T(8,128)}, f32[96,3072]{1,0:T(8,128)}, f32[384,768]{1,0:T(8,128)}) async-done(((f32[96,2304]{1,0:T(8,128)}, f32[96,768]{1,0:T(8,128)}, f32[96,3072]{1,0:T(8,128)}, f32[384,768]{1,0:T(8,128)}), (f32[96,2304]{1,0:T(8,128)}, f32[96,768]{1,0:T(8,128)}, f32[96,3072]{1,0:T(8,128)}, ...) | async-done | bytes 3538960 | tf_op jit(solution)/shard_map/psum | solution.py:243
  849.5 4.7 multiply_reduce_fusion.7
  854.3 2.9 multiply_reduce_fusion.6
  866.8 30.4 %all-reduce.8 = (f32[10752]{0:T(1024)}, f32[4]{0:T(128)S(1)}, f32[4]{0:T(128)S(1)}) all-reduce(f32[10752]{0:T(1024)} %copy-done.59, f32[4]{0:T(128)S(1)} %pad_maximum_fusion.1, f32[4]{0:T(128)S(1)} %pad_maximum_fusion.2), channel_id=6, replica_groups=mesh['dp'=4,'fsdp'=8] {'fsdp'}, use_global_device_ids=true, to_apply=%region_33.34.clone | all-reduce | flops 10760 | bytes 86080
  904.5 9.1 psum.60
  913.6 3.4 multiply_subtract_fusion
  (419 shorter events, 274.8 us)
Async XLA Ops:
  7.2 4.0 copy-start.17
  7.2 5.0 copy-start.15
  7.2 47.8 %all-gather.5.cloned.1.call-start = ((), (), s32[]{:S(2)}) async-start(), calls=%async_computation.4 | async-start | bytes 3981312 | tf_op jit(solution)/shard_map/all_gather | solution.py:132
  9.4 3.7 copy-start.65
  9.4 3.8 copy-start.80
  9.4 200.0 %all-gather.7.cloned.1.call-start = ((), (), s32[]{:S(2)}) async-start(), calls=%async_computation.5 | async-start | bytes 1327104 | tf_op jit(solution)/shard_map/all_gather | solution.py:133
  11.1 203.8 %all-gather.9.cloned.1.call-start = ((), (), s32[]{:S(2)}) async-start(), calls=%async_computation.6 | async-start | bytes 5308416 | tf_op jit(solution)/shard_map/all_gather | solution.py:134
  12.1 34.8 %copy-start.33 = (bf16[1024,768]{1,0:T(8,128)(2,1)S(1)}, bf16[1024,768]{1,0:T(8,128)(2,1)}, u32[]{:S(2)}) copy-start(bf16[1024,768]{1,0:T(8,128)(2,1)} %param.23) | copy-start | bytes 4718596
  12.1 240.6 %all-gather.11.cloned.1.call-start = ((), (), s32[]{:S(2)}) async-start(), calls=%async_computation.7 | async-start | bytes 5308416 | tf_op jit(solution)/shard_map/all_gather | solution.py:135
  13.1 507.0 %reduce-scatter.7.cloned.1.call-start = ((), (), s32[]{:S(2)}) async-start(), calls=%async_computation.9 | async-start | bytes 2654208 | tf_op jit(solution)/shard_map/reduce_scatter | solution.py:238
  46.8 8.3 copy-start.56
  46.8 8.3 copy-start.76
  47.7 161.8 %copy-start.1 = (bf16[1024,768]{0,1:T(8,128)(2,1)}, bf16[1024,768]{0,1:T(8,128)(2,1)S(1)}, u32[]{:S(2)}) copy-start(bf16[1024,768]{0,1:T(8,128)(2,1)S(1)} %copy.82) | copy-start | bytes 4718596
  48.0 13.4 %copy-start.50 = (f32[1024]{0:T(1024)}, f32[1024]{0:T(1024)S(1)}, u32[]{:S(2)}) copy-start(f32[1024]{0:T(1024)S(1)} %broadcast_multiply_fusion.1) | copy-start | bytes 12292
  48.5 12.9 %copy-start.60 = (f32[1024]{0:T(1024)}, f32[1024]{0:T(1024)S(1)}, u32[]{:S(2)}) copy-start(f32[1024]{0:T(1024)S(1)} %fusion.88) | copy-start | bytes 12292
  48.5 23.2 %copy-start.46 = (f32[12,32]{1,0:T(8,128)}, f32[12,32]{1,0:T(8,128)S(1)}, u32[]{:S(2)}) copy-start(f32[12,32]{1,0:T(8,128)S(1)} %slice.124) | copy-start | bytes 4612
  49.1 22.7 %copy-start.48 = (f32[12,32]{1,0:T(8,128)}, f32[12,32]{1,0:T(8,128)S(1)}, u32[]{:S(2)}) copy-start(f32[12,32]{1,0:T(8,128)S(1)} %slice.127) | copy-start | bytes 4612
  49.1 22.7 %copy-start.52 = (f32[1,1024]{1,0:T(1,128)}, f32[1,1024]{1,0:T(1,128)S(1)}, u32[]{:S(2)}) copy-start(f32[1,1024]{1,0:T(1,128)S(1)} %get-tuple-element.387) | copy-start | bytes 12292
  49.1 22.7 %copy-start.54 = (f32[1,1024]{1,0:T(1,128)}, f32[1,1024]{1,0:T(1,128)S(1)}, u32[]{:S(2)}) copy-start(f32[1,1024]{1,0:T(1,128)S(1)} %get-tuple-element.388) | copy-start | bytes 12292
  214.9 37.8 %copy-start.11 = (bf16[1024,768]{0,1:T(8,128)(2,1)S(1)}, bf16[1024,768]{0,1:T(8,128)(2,1)}, u32[]{:S(2)}) copy-start(bf16[1024,768]{0,1:T(8,128)(2,1)} %copy.90) | copy-start | bytes 4718596
  214.9 37.8 %copy-start.64 = (f32[1024]{0:T(1024)S(1)}, f32[1024]{0:T(1024)}, u32[]{:S(2)}) copy-start(f32[1024]{0:T(1024)} %compare_convert_fusion) | copy-start | bytes 12292
  281.2 3.7 copy-start.6
  294.7 257.3 %reduce-scatter.5.cloned.1.call-start = ((), (), s32[]{:S(2)}) async-start(), calls=%async_computation.8 | async-start | bytes 7962624 | tf_op jit(solution)/shard_map/reduce_scatter | solution.py:237
  300.4 144.8 %copy-start.4 = (f32[1024,768]{0,1:T(8,128)S(1)}, f32[1024,768]{0,1:T(8,128)}, u32[]{:S(2)}) copy-start(f32[1024,768]{0,1:T(8,128)} %copy.83) | copy-start | bytes 9437188
  300.4 144.8 %copy-start.47 = (f32[12,32]{1,0:T(8,128)S(1)}, f32[12,32]{1,0:T(8,128)}, u32[]{:S(2)}) copy-start(f32[12,32]{1,0:T(8,128)} %copy-done.46) | copy-start | bytes 4612
  300.4 144.8 %copy-start.49 = (f32[12,32]{1,0:T(8,128)S(1)}, f32[12,32]{1,0:T(8,128)}, u32[]{:S(2)}) copy-start(f32[12,32]{1,0:T(8,128)} %copy-done.48) | copy-start | bytes 4612
  300.4 144.8 %copy-start.53 = (f32[1,1024]{1,0:T(1,128)S(1)}, f32[1,1024]{1,0:T(1,128)}, u32[]{:S(2)}) copy-start(f32[1,1024]{1,0:T(1,128)} %copy-done.52) | copy-start | bytes 12292
  300.4 144.8 %copy-start.55 = (f32[1,1024]{1,0:T(1,128)S(1)}, f32[1,1024]{1,0:T(1,128)}, u32[]{:S(2)}) copy-start(f32[1,1024]{1,0:T(1,128)} %copy-done.54) | copy-start | bytes 12292
  457.5 8.6 copy-start.20
  476.0 176.2 %reduce-scatter.9.cloned.1.call-start = ((), (), s32[]{:S(2)}) async-start(), calls=%async_computation.10 | async-start | bytes 10616832 | tf_op jit(solution)/shard_map/reduce_scatter | solution.py:239
  486.6 265.8 %reduce-scatter.11.cloned.1.call-start = ((), (), s32[]{:S(2)}) async-start(), calls=%async_computation.11 | async-start | bytes 10616832 | tf_op jit(solution)/shard_map/reduce_scatter | solution.py:240
  498.2 351.3 %all-reduce.12.cloned.1.call-start = ((), (), s32[]{:S(2)}) async-start(), calls=%async_computation.12 | async-start | bytes 7077888 | tf_op jit(solution)/shard_map/psum | solution.py:243
  764.8 40.8 %copy-start.58 = (f32[10752]{0:T(1024)S(1)}, f32[10752]{0:T(1024)}, u32[]{:S(2)}) copy-start(f32[10752]{0:T(1024)} %custom-call) | copy-start | bytes 129028
  764.9 40.8 %copy-start.79 = (f32[768]{0:T(1024)S(1)}, f32[768]{0:T(1024)}, u32[]{:S(2)}) copy-start(f32[768]{0:T(1024)} %get-tuple-element.402) | copy-start | bytes 9220
  764.9 40.8 %copy-start.68 = (f32[768]{0:T(1024)S(1)}, f32[768]{0:T(1024)}, u32[]{:S(2)}) copy-start(f32[768]{0:T(1024)} %get-tuple-element.288) | copy-start | bytes 9220
  764.9 40.8 %copy-start.78 = (f32[768]{0:T(1024)S(1)}, f32[768]{0:T(1024)}, u32[]{:S(2)}) copy-start(f32[768]{0:T(1024)} %get-tuple-element.404) | copy-start | bytes 9220
  767.5 41.1 %copy-start.69 = (f32[3072]{0:T(1024)S(1)}, f32[3072]{0:T(1024)}, u32[]{:S(2)}) copy-start(f32[3072]{0:T(1024)} %get-tuple-element.406) | copy-start | bytes 36868
  767.5 82.0 %copy-start.18 = (f32[96,3072]{1,0:T(8,128)S(1)}, f32[96,3072]{1,0:T(8,128)}, u32[]{:S(2)}) copy-start(f32[96,3072]{1,0:T(8,128)} %param.29) | copy-start | bytes 3538948
  767.5 82.0 %copy-start.39 = (f32[96,3072]{1,0:T(8,128)S(1)}, f32[96,3072]{1,0:T(8,128)}, u32[]{:S(2)}) copy-start(f32[96,3072]{1,0:T(8,128)} %param.34) | copy-start | bytes 3538948
  808.6 40.9 %copy-start.59 = (f32[10752]{0:T(1024)}, f32[10752]{0:T(1024)S(1)}, u32[]{:S(2)}) copy-start(f32[10752]{0:T(1024)S(1)} %constant_dynamic-update-slice_fusion) | copy-start | bytes 129028
  849.5 4.8 copy-start.16
  849.5 4.8 copy-start.24
  849.5 4.8 copy-start.40
  849.5 4.7 copy-start.41
  897.2 6.4 copy-start.73
  897.8 5.8 copy-start.74
  913.5 7.5 copy-start.67
  918.7 3.9 copy-start.36
  (54 other events, 124.6 us)
Sparse Core Ops, SparseCore 0:
  10.3 44.7 all-gather.4
  57.3 21.5 all-gather.6
  81.0 51.4 all-gather.8
  134.6 50.5 all-gather.10
  294.9 34.8 reduce-scatter.6
  476.1 75.8 reduce-scatter.4
  554.3 97.8 reduce-scatter.8
  654.5 97.8 reduce-scatter.10
  755.9 93.5 all-reduce.11
where the time goes:
time: 943 us; the launch traced here: 932 us
  matrix products  338 us (36%)
  waiting for transfers between devices  277 us (29%)
  blocking collectives  109 us (12%)
  other arithmetic  99.2 us (11%)
  local copies, waits for them, and re-layouts  86 us (9%)
  between operations  21.8 us (2%)
    dot_general x40, matrix products, against_columns(): lax.dot_general(left, right, (((1,), (1,)), ((), ())), preferred_element_...  114 us
    reduce_scatter x1, waiting for transfers between devices, body(): lax.psum_scatter(up_grad, 'fsdp', scatter_dimension=0, tiled=True)  100 us
    reduce_scatter x1, waiting for transfers between devices, body(): lax.psum_scatter(down_grad, 'fsdp', scatter_dimension=0, tiled=True)  100 us
    dot_general x28, matrix products, across_rows(): lax.dot_general(left, right, (((0,), (0,)), ((), ())), preferred_element_...  89.7 us
    unnamed x2, blocking collectives  61.9 us
    dot_general x12, matrix products, attend_forward(): jnp.dot(probs, value_rows, preferred_element_type=jnp.float32)  51.1 us
    psum x1, waiting for transfers between devices, body(): lax.psum((group_grads[0], group_grads[1], group_grads[2], group_grads[3],...  40.9 us
    psum x1, blocking collectives, body(): down_bias_grad = lax.psum(grad_bias_down, ('dp', 'fsdp'))  38.1 us
  transfers between devices with their start and end apart: 9, of which 5 were waited for; matrix products, arithmetic and copies ran while one was open for 45% of the time, Pallas kernels for 0%

commit v1 on v0

--- a/solution.py
+++ b/solution.py
@@ -97,7 +97,105 @@
     return (first_new, second_new, update)
 
 
+def px(x): return lax.ppermute(x,"dp",[(i,i^1) for i in range(4)])
+def py(x): return lax.ppermute(x,"dp",[(i,i^2) for i in range(4)])
+def pd(x): return lax.ppermute(x,"dp",[(i,i^3) for i in range(4)])
+def pc(x): return lax.ppermute(x,"fsdp",[(i,i^1) for i in range(8)])
+def pz(x,s): return lax.ppermute(x,"fsdp",[(i,(i+2*s)%8) for i in range(8)])
+def place():
+    d=lax.axis_index("dp"); f=lax.axis_index("fsdp")
+    return d%2, d//2, f//2, f%2
+def pick(flag,a,b):
+    return jnp.where(flag==0,a,b)
+def order_z(own, got, z):
+    out=[]
+    cand=[own]+got
+    for k in range(4):
+        rel=(z-k)%4
+        v=cand[3]
+        for s in (2,1,0): v=jnp.where(rel==s,cand[s],v)
+        out.append(v)
+    return out
+def gather(shard):
+    x,y,z,c=place()
+    r,C=shard.shape
+    h,w=r//2,C//2
+    part=lax.dynamic_slice(shard,(x*h,y*w),(h,w))
+    got=[pz(part,s) for s in (1,2,3)]
+    Z=jnp.stack(order_z(part,got,z))
+    zx=px(Z); zy=py(Z)
+    fy=py(zx[:2]); fx=px(zy[2:])
+    zd=jnp.concatenate([fy,fx],0)
+    top=jnp.concatenate([pick(y,pick(x,Z,zx),pick(x,zy,zd)),pick(y,pick(x,zy,zd),pick(x,Z,zx))],2)
+    bot=jnp.concatenate([pick(y,pick(x,zx,Z),pick(x,zd,zy)),pick(y,pick(x,zd,zy),pick(x,zx,Z))],2)
+    full=jnp.concatenate([top,bot],1)
+    other=pc(full)
+    both=jnp.stack([pick(c,full,other),pick(c,other,full)],1)
+    return both.reshape(8*r,C)
+def rnd(v): return v.astype(jnp.bfloat16)
+def up(v): return v.astype(jnp.float32)
+def reduce(G):
+    x,y,z,c=place()
+    R,C=G.shape; r=R//8; h,w=r//2,C//2
+    G=G.reshape(4,2,r,C)
+    mine=pick(c,G[:,0],G[:,1]); theirs=pick(c,G[:,1],G[:,0])
+    S=rnd(up(mine)+up(pc(theirs)))
+    q=lambda a,b: lax.dynamic_slice(S,(0,a*h,b*w),(4,h,w))
+    own,qx,qy,qd=q(x,y),q(1-x,y),q(x,1-y),q(1-x,1-y)
+    d0=px(qd[:2]); d1=py(qd[2:])
+    sx=jnp.concatenate([qx[:2],rnd(up(qx[2:])+up(d1))],0)
+    sy=jnp.concatenate([rnd(up(qy[:2])+up(d0)),qy[2:]],0)
+    gx=px(sx); gy=py(sy)
+    D=rnd(up(own)+up(gx)+up(gy))
+    send=lambda s: lax.dynamic_index_in_dim(D,(z+s)%4,0,keepdims=False)
+    got=[pz(send(s),s) for s in (1,2,3)]
+    F=rnd(up(send(0))+up(got[0])+up(got[1])+up(got[2]))
+    rx,ry,rd=px(F),py(F),pd(F)
+    tl=pick(y,pick(x,F,rx),pick(x,ry,rd)); tr=pick(y,pick(x,ry,rd),pick(x,F,rx))
+    bl=pick(y,pick(x,rx,F),pick(x,rd,ry)); br=pick(y,pick(x,rd,ry),pick(x,rx,F))
+    return up(jnp.concatenate([jnp.concatenate([tl,tr],1),jnp.concatenate([bl,br],1)],0))
+
+
+def sum_z(v):
+    x, y, z, c = place()
+    got = [pz(v, s) for s in (1, 2, 3)]
+    a = order_z(v, got, z)
+    return (a[0] + a[1]) + (a[2] + a[3])
+
+
+def total_fsdp(v):
+    return sum_z(v + pc(v))
+
+
+def total_all(v):
+    v = v + pc(v)
+    v = v + px(v)
+    v = v + py(v)
+    return sum_z(v)
+
+
+def gather_vector(shard):
+    x, y, z, c = place()
+    row = shard.reshape(1, -1)
+    rows = jnp.stack(order_z(row, [pz(row, s) for s in (1, 2, 3)], z))
+    other = pc(rows)
+    return jnp.stack([pick(c, rows, other), pick(c, other, rows)], 1).reshape(-1)
+
+
+def reduce_vector(v):
+    x, y, z, c = place()
+    v = v.reshape(4, 2, -1)
+    v = v + pc(v)
+    v = v + px(v)
+    v = v + py(v)
+    v = pick(c, v[:, 0], v[:, 1])
+    send = lambda s: lax.dynamic_index_in_dim(v, (z + s) % 4, 0, keepdims=True)
+    got = [pz(send(s), s) for s in (1, 2, 3)]
+    return (send(0) + got[0] + got[1] + got[2]).reshape(-1)
+
+
 def body(
+    mesh_fast,
     tokens,
     cotangent,
     image_ids,
@@ -128,13 +226,19 @@
     low_up = up_weight.astype(jnp.bfloat16)
     low_down = down_weight.astype(jnp.bfloat16)
     low_vectors = vectors.astype(jnp.bfloat16)
-    full_qkv, full_out, full_up, full_down, full_vectors = (
-        lax.all_gather(low_qkv, "fsdp", axis=0, tiled=True),
-        lax.all_gather(low_out, "fsdp", axis=0, tiled=True),
-        lax.all_gather(low_up, "fsdp", axis=0, tiled=True),
-        lax.all_gather(low_down, "fsdp", axis=0, tiled=True),
-        lax.all_gather(low_vectors, "fsdp", axis=0, tiled=True),
-    )
+    if mesh_fast:
+        get, get_vector, give, give_vector = gather, gather_vector, reduce, reduce_vector
+        over_fsdp, over_all = total_fsdp, total_all
+    else:
+        get = get_vector = lambda v: lax.all_gather(v, "fsdp", axis=0, tiled=True)
+        give = lambda v: lax.psum(
+            lax.psum_scatter(up(v), "fsdp", scatter_dimension=0, tiled=True), "dp"
+        )
+        give_vector = give
+        over_fsdp = lambda v: lax.psum(v, "fsdp")
+        over_all = lambda v: lax.psum(v, ("dp", "fsdp"))
+    full_vectors = get_vector(low_vectors)
+    full_qkv, full_out, full_up, full_down = get(low_qkv), get(low_out), get(low_up), get(low_down)
     gain_one, shift_one, gain_two, shift_two, bias_qkv, bias_out, bias_up, bias_down, freq_flat = (
         split_vector(full_vectors.astype(jnp.float32), width, hidden_width)
     )
@@ -173,16 +277,11 @@
     output = (
         resid + jnp.dot(active, full_down, preferred_element_type=jnp.float32) + bias_down
     ).astype(jnp.bfloat16)
-    back_qkv, back_out, back_up, back_down = (
-        lax.all_gather(low_qkv, "fsdp", axis=0, tiled=True),
-        lax.all_gather(low_out, "fsdp", axis=0, tiled=True),
-        lax.all_gather(low_up, "fsdp", axis=0, tiled=True),
-        lax.all_gather(low_down, "fsdp", axis=0, tiled=True),
-    )
+    back_qkv, back_out, back_up, back_down = full_qkv, full_out, full_up, full_down
     given_low = given.astype(jnp.bfloat16)
     down_grad = across_rows(active, given_low)
     grad_bias_down = jnp.sum(given, axis=0)
-    down_bias_grad = lax.psum(grad_bias_down, ("dp", "fsdp"))
+    down_bias_grad = over_all(grad_bias_down.reshape(1, -1)).reshape(-1)
     grad_active = against_columns(given_low, back_down)
     unused_gelu, gelu_pull = jax.vjp(exact_gelu, hidden)
     grad_hidden = gelu_pull(grad_active)[0].astype(jnp.bfloat16)
@@ -233,15 +332,12 @@
             grad_freqs.reshape(-1),
         ]
     )
-    group_grads = (
-        lax.psum_scatter(qkv_grad, "fsdp", scatter_dimension=0, tiled=True),
-        lax.psum_scatter(out_grad, "fsdp", scatter_dimension=0, tiled=True),
-        lax.psum_scatter(up_grad, "fsdp", scatter_dimension=0, tiled=True),
-        lax.psum_scatter(down_grad, "fsdp", scatter_dimension=0, tiled=True),
-        lax.psum_scatter(vector_grad, "fsdp", scatter_dimension=0, tiled=True),
-    )
-    reduced = lax.psum(
-        (group_grads[0], group_grads[1], group_grads[2], group_grads[3], group_grads[4]), "dp"
+    reduced = (
+        give(rnd(qkv_grad)),
+        give(rnd(out_grad)),
+        give(rnd(up_grad)),
+        give(rnd(down_grad)),
+        give_vector(vector_grad),
     )
     firsts = (qkv_first, out_first, up_first, down_first)
     seconds = (qkv_second, out_second, up_second, down_second)
@@ -257,7 +353,8 @@
         update_list.append(update)
     update_local = jnp.stack([jnp.sum(update * update) for update in update_list])
     weight_local = jnp.stack([jnp.sum(matrix * matrix) for matrix in masters])
-    weight_squares, update_squares = lax.psum((weight_local, update_local), "fsdp")
+    weight_squares = over_fsdp(weight_local.reshape(1, -1)).reshape(-1)
+    update_squares = over_fsdp(update_local.reshape(1, -1)).reshape(-1)
     weight_norms = jnp.sqrt(weight_squares)
     update_norms = jnp.sqrt(update_squares)
     new_list = []
@@ -346,4 +443,5 @@
         P(),
         P(),
     )
-    return jax.shard_map(body, mesh=mesh, in_specs=in_specs, out_specs=out_specs, check_vma=False)
+    fast = mesh.shape["dp"] == 4 and mesh.shape["fsdp"] == 8
+    return jax.shard_map(partial(body, fast), mesh=mesh, in_specs=in_specs, out_specs=out_specs, check_vma=False)

time: 943 us -> 823 us (0.87)
  waiting for transfers between devices: 277 us -> 93.6 us
  starting transfers between devices: 0.37 us -> 127 us
  blocking collectives: 109 us -> 0 us
  local copies, waits for them, and re-layouts: 86 us -> 125 us
  other arithmetic: 99.2 us -> 135 us
  matrix products: 338 us -> 322 us
  between operations: 21.8 us -> 8.23 us
    reduce_scatter x4 -> x0, waiting for transfers between devices: 232 us -> none  [the longest x1 100 us: body(): lax.psum_scatter(up_grad, 'fsdp', scatter_dimension=0, tiled=True)]
    ppermute x0 -> x100, starting transfers between devices: none -> 127 us  [the longest x39 68.1 us: pz(): return lax.ppermute(x, 'fsdp', [(i, (i + 2 * s) % 8) for i in range(8)])]
    ppermute x0 -> x100, waiting for transfers between devices: none -> 93.6 us  [the longest x22 37.5 us: px(): return lax.ppermute(x, 'dp', [(i, i ^ 1) for i in range(4)])]
    unnamed x2 -> x0, blocking collectives: 61.9 us -> none
    psum x2 -> x0, blocking collectives: 47.2 us -> none  [the longest x1 38.1 us: body(): down_bias_grad = lax.psum(grad_bias_down, ('dp', 'fsdp'))]
    psum x1 -> x0, waiting for transfers between devices: 40.9 us -> none  [body(): lax.psum((group_grads[0], group_grads[1], group_grads[2], group_grads[3],...]
    dynamic_update_slice x12, local copies, waits for them, and re-layouts: 1.32 us -> 16.8 us  [body(): lax.map(partial(attend_forward, same_image=same_image, scale=scale), (que...]
    another operation x8 -> x25, other arithmetic: 16.6 us -> 26.6 us
  transfers between devices with their start and end apart: 9 -> 100, of which waited for: 5 -> 40; matrix products, arithmetic and copies ran while one was open for 45% -> 30% of each run, Pallas kernels for 0% -> 0%
where the time goes in v1:
time: 823 us; the launch traced here: 811 us
  matrix products  322 us (39%)
  other arithmetic  135 us (16%)
  starting transfers between devices  127 us (15%)
  local copies, waits for them, and re-layouts  125 us (15%)
  waiting for transfers between devices  93.6 us (11%)
  between operations  8.23 us (1%)
    dot_general x40, matrix products, against_columns(): lax.dot_general(left, right, (((1,), (1,)), ((), ())), preferred_element_...  108 us
    dot_general x28, matrix products, across_rows(): lax.dot_general(left, right, (((0,), (0,)), ((), ())), preferred_element_...  84.6 us
    ppermute x39, starting transfers between devices, pz(): return lax.ppermute(x, 'fsdp', [(i, (i + 2 * s) % 8) for i in range(8)])  68.1 us
    dot_general x12, matrix products, attend_forward(): jnp.dot(probs, value_rows, preferred_element_type=jnp.float32)  50.3 us
    unnamed x235, local copies, waits for them, and re-layouts  39.1 us
    ppermute x22, waiting for transfers between devices, px(): return lax.ppermute(x, 'dp', [(i, i ^ 1) for i in range(4)])  37.5 us
    dot_general x1, matrix products, body(): jnp.dot(normed_two, full_up, preferred_element_type=jnp.float32) + bias_up  35.9 us
    ppermute x22, waiting for transfers between devices, py(): return lax.ppermute(x, 'dp', [(i, i ^ 2) for i in range(4)])  29 us
  transfers between devices with their start and end apart: 100, of which 40 were waited for; matrix products, arithmetic and copies ran while one was open for 30% of the time, Pallas kernels for 0%

profile of v1, /device:TPU:0, one launch (start us, length us, event | category | flops | bytes accessed | tf_op | source)
XLA Modules:
  0.0 810.5 jit_solution(14529764903352814250)
XLA Ops:
  41.7 3.4 collective-permute-start.30
  45.1 5.3 collective-permute-done.21
  63.3 8.2 %collective-permute-done.17 = bf16[2,48,384]{2,1,0:T(8,128)(2,1)S(1)} collective-permute-done((bf16[2,48,384]{2,1,0:T(8,128)(2,1)S(1)}, bf16[2,48,384]{2,1,0:T(8,128)(2,1)S(1)}, u32[]{:S(2)}, u32[]{:S(2)}) %collective-permute-start.17) | collective-permute-done | bytes 73760 | tf_op jit(solution)/shard_map/ppermute | solution.py:101
  72.9 7.3 collective-permute-done.18
  85.6 10.6 %collective-permute-done.31 = bf16[4,192,384]{2,1,0:T(8,128)(2,1)S(1)} collective-permute-done((bf16[4,192,384]{2,1,0:T(8,128)(2,1)S(1)}, bf16[4,192,384]{2,1,0:T(8,128)(2,1)S(1)}, u32[]{:S(2)}, u32[]{:S(2)}) %collective-permute-start.31) | collective-permute-done | bytes 589856 | tf_op jit(solution)/shard_map/ppermute | solution.py:100
  117.4 4.3 convolution_add_fusion
  124.8 3.6 copy.109
  128.4 3.5 copy.111
  131.9 10.8 %subtract_convert_fusion = (bf16[1024,12,32]{0,2,1:T(8,128)(2,1)S(1)}, bf16[1024,12,32]{0,2,1:T(8,128)(2,1)S(1)}, bf16[1024,12,32]{0,2,1:T(8,128)(2,1)S(1)}, bf16[1024,12,32]{0,2,1:T(8,128)(2,1)S(1)}) fusion(f32[1024,12,64]{0,2,1:T(8,128)} %bitcast.356, f32[12,32]{1,0:T(8,128)S(1)} %get-tuple-element.451, f32[1024]{0:T(1024)S(1)} %bitcast.397, ...), kind=kLoop, calls=%fused_computation.156 | loop fusion | flops 7471104 | bytes 9448448 | tf_op jit(solution)/shard_map/convert.18
  144.9 4.1 copy.113
  149.0 4.2 copy.114
  154.8 4.1 copy.115
  159.0 125.7 %while.28 = (s32[]{:T(128)}, bf16[12,1024,64]{1,2,0:T(8,128)(2,1)}, f32[12,1024]{1,0:T(8,128)}, bf16[12,1024,64]{2,1,0:T(8,128)(2,1)}, bf16[12,1024,64]{2,1,0:T(...) while((s32[]{:T(128)}, bf16[12,1024,64]{1,2,0:T(8,128)(2,1)}, ...), condition=%wide.region_5.6_spmd.clone, body=%wide.region_2.5_spmd.clone.sunk | while | flops 284228608 | bytes 30341244 | solution.py:268
  165.3 4.2 fusion.189
  175.8 4.2 fusion.189
  186.2 4.2 fusion.189
  196.7 4.2 fusion.189
  207.1 4.2 fusion.189
  217.6 4.2 fusion.189
  228.1 4.2 fusion.189
  238.5 4.2 fusion.189
  249.0 4.2 fusion.189
  259.4 4.2 fusion.189
  269.9 4.2 fusion.189
  280.4 4.2 fusion.189
  300.1 35.9 %multiply_convert_fusion = (bf16[1024,3072]{1,0:T(8,128)(2,1)}, f32[1024,3072]{1,0:T(8,128)}, f32[1024,3072]{1,0:T(8,128)}) fusion(f32[3072]{0:T(1024)S(1)} %slice.335, bf16[768,3072]{1,0:T(8,128)(2,1)S(1)} %bitcast.384, f32[1024,768]{0,1:T(8,128)S(1)} %get-tuple-element.492, f32[768]{0:T(1024)S(1)} %get-tuple-element.464, f32[768]{0:T(1024)S(1)} %get-tuple-element.465, ...), kind=kOutput, calls=%fused_computation.64 | convolution fusion | flops 5043388416 | bytes 39348224 | tf_op jit(solution)/shard_map/dot_general | solution.py:275
  335.9 17.7 %convert_reduce_fusion = (f32[3072]{0:T(1024)}, bf16[1024,3072]{1,0:T(8,128)(2,1)}) fusion(f32[1024,3072]{1,0:T(8,128)} %get-tuple-element.356, bf16[3072,768]{1,0:T(8,128)(2,1)} %bitcast.382, bf16[1024,768]{0,1:T(8,128)(2,1)S(1)} %copy-done.12, f32[1024]{0:T(1024)S(1)} %copy-done.81, f32[1024,3072]{1,0:T(8,128)} %get-tuple-element.493, f32[3072]{0:T(1024)S(1)} %slice.335), kind=kOutput, calls=%fused_computation.62 | convolution fusion | flops 4887671808 | bytes 37777408 | tf_op jit(solution)/shard_map/dot_general | solution.py:60
  353.7 9.9 %convolution_convert_fusion.1 = bf16[768,3072]{1,0:T(8,128)(2,1)} fusion(bf16[1024,3072]{1,0:T(8,128)(2,1)} %get-tuple-element.499, f32[1024,768]{0,1:T(8,128)S(1)} %get-tuple-element.492, f32[768]{0:T(1024)S(1)} %get-tuple-element.464, f32[768]{0:T(1024)S(1)} %get-tuple-element.465, f32[1024]{0:T(1024)S(1)} %fusion.116, f32[1024]{0:T(1024)S(1)} %broadcast_multiply_fusion), kind=kOutput, calls=%fused_computation.81 | convolution fusion | flops 4838129664 | bytes 14170112 | tf_op jit(solution)/shard_map/dot_general | solution.py:54
  363.6 7.3 fusion.148
  370.9 4.1 copy.121
  375.1 3.5 multiply_reduce_fusion.1
  388.7 153.6 %while.29 = (s32[]{:T(128)}, f32[12,1024,64]{1,2,0:T(8,128)}, f32[12,1024,64]{1,2,0:T(8,128)}, bf16[12,1024,64]{1,2,0:T(8,128)(2,1)}, bf16[12,1024,64]{2,1,0:T(8...) while((s32[]{:T(128)}, f32[12,1024,64]{1,2,0:T(8,128)}, ...), condition=%wide.region_12.13_spmd.clone, body=%wide.region_10.12_spmd.clone.sunk | while | flops 683801600 | bytes 34116720 | solution.py:299
  542.3 12.2 %multiply_add_fusion = (f32[1024,12,32]{0,2,1:T(8,128)S(1)}, f32[1024,12,32]{0,2,1:T(8,128)S(1)}, f32[1024,12,32]{0,2,1:T(8,128)S(1)}, f32[1024,12,32]{0,2,1:T(8,128)S(1)}) fusion(f32[1024,12,64]{0,2,1:T(8,128)} %bitcast.370, f32[1024,12,64]{0,2,1:T(8,128)} %bitcast.388, f32[1024,12,64]{0,2,1:T(8,128)} %bitcast.357, f32[1024,12,64]{0,2,1:T(8,128)S(1)} %bitcast.355, ...), kind=kLoop, calls=%fused_computation.150 | loop fusion | flops 13762560 | bytes 18885632 | tf_op jit(solution)/shard_map/transpose(jvp())/add_any | solution.py:28
  554.5 6.7 multiply_reduce_fusion.5
  563.1 7.5 convolution_convert_fusion.2
  570.6 7.8 fusion.147
  580.5 6.9 convolution_convert_fusion
  590.4 3.8 copy.126
  602.5 9.7 %add_convert_fusion.4 = bf16[1024,768]{0,1:T(8,128)(2,1)} fusion(f32[1024,768]{0,1:T(8,128)S(1)} %copy-done.7, bf16[1024,3072]{1,0:T(8,128)(2,1)} %get-tuple-element.355, bf16[3072,768]{1,0:T(8,128)(2,1)} %bitcast.383, f32[768]{0:T(1024)S(1)} %copy-done.94), kind=kOutput, calls=%fused_computation.121 | convolution fusion | flops 4834197504 | bytes 15731712 | tf_op jit(solution)/shard_map/dot_general | solution.py:278
  635.8 3.4 collective-permute-start.90
  641.0 4.1 select_bitcast_fusion
  674.2 4.2 collective-permute-start.54
  704.0 3.9 collective-permute-done.38
  735.4 5.9 collective-permute-done.71
  749.6 4.7 collective-permute-start.64
  754.5 4.2 collective-permute-done.75
  758.9 3.4 collective-permute-start.79
  783.9 3.9 collective-permute-start.97
  (744 shorter events, 511.0 us)
Async XLA Ops:
  2.2 24.2 %collective-permute-start.12 = (bf16[48,384]{1,0:T(8,128)(2,1)}, bf16[48,384]{1,0:T(8,128)(2,1)S(1)}, u32[]{:S(2)}, u32[]{:S(2)}) collective-permute-start(bf16[48,384]{1,0:T(8,128)(2,1)} %dynamic_slice.303), channel_id=1, source_target_pairs={{0,2},{1,3},{2,4},{3,5},{4,6},{5,7},{6,0},{7,1},{8,10},{9,11},{10,... | collective-permute-start | bytes 110600 | tf_op jit(solution)/shard_map/ppermute | solution.py:104
  5.2 22.2 %collective-permute-start.13 = (bf16[48,384]{1,0:T(8,128)(2,1)}, bf16[48,384]{1,0:T(8,128)(2,1)S(1)}, u32[]{:S(2)}, u32[]{:S(2)}) collective-permute-start(bf16[48,384]{1,0:T(8,128)(2,1)} %dynamic_slice.303), channel_id=1, source_target_pairs={{0,4},{1,5},{2,6},{3,7},{4,0},{5,1},{6,2},{7,3},{8,12},{9,13},{10,... | collective-permute-start | bytes 110600 | tf_op jit(solution)/shard_map/ppermute | solution.py:104
  16.7 11.8 %collective-permute-start.14 = (bf16[48,384]{1,0:T(8,128)(2,1)}, bf16[48,384]{1,0:T(8,128)(2,1)}, u32[]{:S(2)}, u32[]{:S(2)}) collective-permute-start(bf16[48,384]{1,0:T(8,128)(2,1)} %dynamic_slice.303), channel_id=1, source_target_pairs={{0,6},{1,7},{2,0},{3,1},{4,2},{5,3},{6,4},{7,5},{8,14},{9,15},{10,... | collective-permute-start | bytes 110600 | tf_op jit(solution)/shard_map/ppermute | solution.py:104
  17.3 13.0 %collective-permute-start.4 = (bf16[48,1152]{1,0:T(8,128)(2,1)S(1)}, bf16[48,1152]{1,0:T(8,128)(2,1)S(1)}, u32[]{:S(2)}, u32[]{:S(2)}) collective-permute-start(bf16[48,1152]{1,0:T(8,128)(2,1)S(1)} %dynamic_slice.302), channel_id=1, source_target_pairs={{0,2},{1,3},{2,4},{3,5},{4,6},{5,7},{6,0},{7,1},{8,10},{9,11},{10,... | collective-permute-start | bytes 331784 | tf_op jit(solution)/shard_map/ppermute | solution.py:104
  26.4 11.2 %collective-permute-start.6 = (bf16[48,1152]{1,0:T(8,128)(2,1)S(1)}, bf16[48,1152]{1,0:T(8,128)(2,1)S(1)}, u32[]{:S(2)}, u32[]{:S(2)}) collective-permute-start(bf16[48,1152]{1,0:T(8,128)(2,1)S(1)} %dynamic_slice.302), channel_id=1, source_target_pairs={{0,6},{1,7},{2,0},{3,1},{4,2},{5,3},{6,4},{7,5},{8,14},{9,15},{10,... | collective-permute-start | bytes 331784 | tf_op jit(solution)/shard_map/ppermute | solution.py:104
  27.4 14.3 %collective-permute-start.20 = (bf16[48,1536]{1,0:T(8,128)(2,1)S(1)}, bf16[48,1536]{1,0:T(8,128)(2,1)S(1)}, u32[]{:S(2)}, u32[]{:S(2)}) collective-permute-start(bf16[48,1536]{1,0:T(8,128)(2,1)S(1)} %dynamic_slice.301), channel_id=1, source_target_pairs={{0,2},{1,3},{2,4},{3,5},{4,6},{5,7},{6,0},{7,1},{8,10},{9,11},{10,... | collective-permute-start | bytes 442376 | tf_op jit(solution)/shard_map/ppermute | solution.py:104
  28.5 22.0 %collective-permute-start.21 = (bf16[48,1536]{1,0:T(8,128)(2,1)S(1)}, bf16[48,1536]{1,0:T(8,128)(2,1)S(1)}, u32[]{:S(2)}, u32[]{:S(2)}) collective-permute-start(bf16[48,1536]{1,0:T(8,128)(2,1)S(1)} %dynamic_slice.301), channel_id=1, source_target_pairs={{0,4},{1,5},{2,6},{3,7},{4,0},{5,1},{6,2},{7,3},{8,12},{9,13},{10,... | collective-permute-start | bytes 442376 | tf_op jit(solution)/shard_map/ppermute | solution.py:104
  30.4 21.6 %collective-permute-start.22 = (bf16[48,1536]{1,0:T(8,128)(2,1)S(1)}, bf16[48,1536]{1,0:T(8,128)(2,1)S(1)}, u32[]{:S(2)}, u32[]{:S(2)}) collective-permute-start(bf16[48,1536]{1,0:T(8,128)(2,1)S(1)} %dynamic_slice.301), channel_id=1, source_target_pairs={{0,6},{1,7},{2,0},{3,1},{4,2},{5,3},{6,4},{7,5},{8,14},{9,15},{10,... | collective-permute-start | bytes 442376 | tf_op jit(solution)/shard_map/ppermute | solution.py:104
  32.9 21.8 %collective-permute-start.28 = (bf16[192,384]{1,0:T(8,128)(2,1)S(1)}, bf16[192,384]{1,0:T(8,128)(2,1)S(1)}, u32[]{:S(2)}, u32[]{:S(2)}) collective-permute-start(bf16[192,384]{1,0:T(8,128)(2,1)S(1)} %dynamic_slice.300), channel_id=1, source_target_pairs={{0,2},{1,3},{2,4},{3,5},{4,6},{5,7},{6,0},{7,1},{8,10},{9,11},{10,... | collective-permute-start | bytes 442376 | tf_op jit(solution)/shard_map/ppermute | solution.py:104
  37.5 19.2 %collective-permute-start.29 = (bf16[192,384]{1,0:T(8,128)(2,1)S(1)}, bf16[192,384]{1,0:T(8,128)(2,1)S(1)}, u32[]{:S(2)}, u32[]{:S(2)}) collective-permute-start(bf16[192,384]{1,0:T(8,128)(2,1)S(1)} %dynamic_slice.300), channel_id=1, source_target_pairs={{0,4},{1,5},{2,6},{3,7},{4,0},{5,1},{6,2},{7,3},{8,12},{9,13},{10,... | collective-permute-start | bytes 442376 | tf_op jit(solution)/shard_map/ppermute | solution.py:104
  41.7 16.6 %collective-permute-start.30 = (bf16[192,384]{1,0:T(8,128)(2,1)S(1)}, bf16[192,384]{1,0:T(8,128)(2,1)S(1)}, u32[]{:S(2)}, u32[]{:S(2)}) collective-permute-start(bf16[192,384]{1,0:T(8,128)(2,1)S(1)} %dynamic_slice.300), channel_id=1, source_target_pairs={{0,6},{1,7},{2,0},{3,1},{4,2},{5,3},{6,4},{7,5},{8,14},{9,15},{10,... | collective-permute-start | bytes 442376 | tf_op jit(solution)/shard_map/ppermute | solution.py:104
  54.7 26.5 %collective-permute-start.7 = (bf16[4,48,1152]{2,1,0:T(8,128)(2,1)S(1)}, bf16[4,48,1152]{2,1,0:T(8,128)(2,1)S(1)}, u32[]{:S(2)}, u32[]{:S(2)}) collective-permute-start(bf16[4,48,1152]{2,1,0:T(8,128)(2,1)S(1)} %pad_maximum_fusion.11), channel_id=1, source_target_pairs={{0,8},{8,0},{16,24},{24,16},{1,9},{9,1},{17,25},{25,17},{2,10},{10... | collective-permute-start | bytes 1327112 | tf_op jit(solution)/shard_map/ppermute | solution.py:100
  56.8 26.1 %collective-permute-start.8 = (bf16[4,48,1152]{2,1,0:T(8,128)(2,1)S(1)}, bf16[4,48,1152]{2,1,0:T(8,128)(2,1)S(1)}, u32[]{:S(2)}, u32[]{:S(2)}) collective-permute-start(bf16[4,48,1152]{2,1,0:T(8,128)(2,1)S(1)} %pad_maximum_fusion.11), channel_id=1, source_target_pairs={{0,16},{8,24},{16,0},{24,8},{1,17},{9,25},{17,1},{25,9},{2,18},{10... | collective-permute-start | bytes 1327112 | tf_op jit(solution)/shard_map/ppermute | solution.py:101
  58.3 25.3 %collective-permute-start.23 = (bf16[4,48,1536]{2,1,0:T(8,128)(2,1)S(1)}, bf16[4,48,1536]{2,1,0:T(8,128)(2,1)S(1)}, u32[]{:S(2)}, u32[]{:S(2)}) collective-permute-start(bf16[4,48,1536]{2,1,0:T(8,128)(2,1)S(1)} %pad_maximum_fusion.5), channel_id=1, source_target_pairs={{0,8},{8,0},{16,24},{24,16},{1,9},{9,1},{17,25},{25,17},{2,10},{10... | collective-permute-start | bytes 1769480 | tf_op jit(solution)/shard_map/ppermute | solution.py:100
  61.7 22.1 %collective-permute-start.24 = (bf16[4,48,1536]{2,1,0:T(8,128)(2,1)S(1)}, bf16[4,48,1536]{2,1,0:T(8,128)(2,1)S(1)}, u32[]{:S(2)}, u32[]{:S(2)}) collective-permute-start(bf16[4,48,1536]{2,1,0:T(8,128)(2,1)S(1)} %pad_maximum_fusion.5), channel_id=1, source_target_pairs={{0,16},{8,24},{16,0},{24,8},{1,17},{9,25},{17,1},{25,9},{2,18},{10... | collective-permute-start | bytes 1769480 | tf_op jit(solution)/shard_map/ppermute | solution.py:101
  80.3 15.9 %collective-permute-start.31 = (bf16[4,192,384]{2,1,0:T(8,128)(2,1)S(1)}, bf16[4,192,384]{2,1,0:T(8,128)(2,1)S(1)}, u32[]{:S(2)}, u32[]{:S(2)}) collective-permute-start(bf16[4,192,384]{2,1,0:T(8,128)(2,1)S(1)} %pad_maximum_fusion.6), channel_id=1, source_target_pairs={{0,8},{8,0},{16,24},{24,16},{1,9},{9,1},{17,25},{25,17},{2,10},{10... | collective-permute-start | bytes 1769480 | tf_op jit(solution)/shard_map/ppermute | solution.py:100
  81.2 16.3 %collective-permute-start.32 = (bf16[4,192,384]{2,1,0:T(8,128)(2,1)S(1)}, bf16[4,192,384]{2,1,0:T(8,128)(2,1)S(1)}, u32[]{:S(2)}, u32[]{:S(2)}) collective-permute-start(bf16[4,192,384]{2,1,0:T(8,128)(2,1)S(1)} %pad_maximum_fusion.6), channel_id=1, source_target_pairs={{0,16},{8,24},{16,0},{24,8},{1,17},{9,25},{17,1},{25,9},{2,18},{10... | collective-permute-start | bytes 1769480 | tf_op jit(solution)/shard_map/ppermute | solution.py:101
  82.9 19.4 %collective-permute-start.9 = (bf16[2,48,1152]{2,1,0:T(8,128)(2,1)S(1)}, bf16[2,48,1152]{2,1,0:T(8,128)(2,1)S(1)}, u32[]{:S(2)}, u32[]{:S(2)}) collective-permute-start(bf16[2,48,1152]{2,1,0:T(8,128)(2,1)S(1)} %slice.316), channel_id=1, source_target_pairs={{0,16},{8,24},{16,0},{24,8},{1,17},{9,25},{17,1},{25,9},{2,18},{10... | collective-permute-start | bytes 663560 | tf_op jit(solution)/shard_map/ppermute | solution.py:101
  83.6 21.4 %collective-permute-start.19 = (bf16[4,96,768]{2,1,0:T(8,128)(2,1)S(1)}, bf16[4,96,768]{2,1,0:T(8,128)(2,1)S(1)}, u32[]{:S(2)}, u32[]{:S(2)}) collective-permute-start(bf16[4,96,768]{2,1,0:T(8,128)(2,1)S(1)} %maximum_maximum_fusion.3), channel_id=1, source_target_pairs={{0,1},{1,0},{2,3},{3,2},{4,5},{5,4},{6,7},{7,6},{8,9},{9,8},{10,11... | collective-permute-start | bytes 1769480 | tf_op jit(solution)/shard_map/ppermute | solution.py:103
  83.7 20.1 %collective-permute-start.10 = (bf16[2,48,1152]{2,1,0:T(8,128)(2,1)S(1)}, bf16[2,48,1152]{2,1,0:T(8,128)(2,1)S(1)}, u32[]{:S(2)}, u32[]{:S(2)}) collective-permute-start(bf16[2,48,1152]{2,1,0:T(8,128)(2,1)S(1)} %slice.317), channel_id=1, source_target_pairs={{0,8},{8,0},{16,24},{24,16},{1,9},{9,1},{17,25},{25,17},{2,10},{10... | collective-permute-start | bytes 663560 | tf_op jit(solution)/shard_map/ppermute | solution.py:100
  96.2 12.4 %collective-permute-start.25 = (bf16[2,48,1536]{2,1,0:T(8,128)(2,1)S(1)}, bf16[2,48,1536]{2,1,0:T(8,128)(2,1)S(1)}, u32[]{:S(2)}, u32[]{:S(2)}) collective-permute-start(bf16[2,48,1536]{2,1,0:T(8,128)(2,1)S(1)} %slice.333), channel_id=1, source_target_pairs={{0,16},{8,24},{16,0},{24,8},{1,17},{9,25},{17,1},{25,9},{2,18},{10... | collective-permute-start | bytes 884744 | tf_op jit(solution)/shard_map/ppermute | solution.py:101
  97.5 11.1 %collective-permute-start.26 = (bf16[2,48,1536]{2,1,0:T(8,128)(2,1)S(1)}, bf16[2,48,1536]{2,1,0:T(8,128)(2,1)S(1)}, u32[]{:S(2)}, u32[]{:S(2)}) collective-permute-start(bf16[2,48,1536]{2,1,0:T(8,128)(2,1)S(1)} %slice.334), channel_id=1, source_target_pairs={{0,8},{8,0},{16,24},{24,16},{1,9},{9,1},{17,25},{25,17},{2,10},{10... | collective-permute-start | bytes 884744 | tf_op jit(solution)/shard_map/ppermute | solution.py:100
  102.3 10.6 %collective-permute-start.33 = (bf16[2,192,384]{2,1,0:T(8,128)(2,1)S(1)}, bf16[2,192,384]{2,1,0:T(8,128)(2,1)S(1)}, u32[]{:S(2)}, u32[]{:S(2)}) collective-permute-start(bf16[2,192,384]{2,1,0:T(8,128)(2,1)S(1)} %slice.336), channel_id=1, source_target_pairs={{0,16},{8,24},{16,0},{24,8},{1,17},{9,25},{17,1},{25,9},{2,18},{10... | collective-permute-start | bytes 884744 | tf_op jit(solution)/shard_map/ppermute | solution.py:101
  111.1 177.1 %collective-permute-start.27 = (bf16[4,96,3072]{2,1,0:T(8,128)(2,1)}, bf16[4,96,3072]{2,1,0:T(8,128)(2,1)}, u32[]{:S(2)}, u32[]{:S(2)}) collective-permute-start(bf16[4,96,3072]{2,1,0:T(8,128)(2,1)} %maximum_maximum_fusion), channel_id=1, source_target_pairs={{0,1},{1,0},{2,3},{3,2},{4,5},{5,4},{6,7},{7,6},{8,9},{9,8},{10,11... | collective-permute-start | bytes 7077896 | tf_op jit(solution)/shard_map/ppermute | solution.py:103
  115.4 178.0 %collective-permute-start.35 = (bf16[4,384,768]{2,1,0:T(8,128)(2,1)}, bf16[4,384,768]{2,1,0:T(8,128)(2,1)}, u32[]{:S(2)}, u32[]{:S(2)}) collective-permute-start(bf16[4,384,768]{2,1,0:T(8,128)(2,1)} %maximum_maximum_fusion.1), channel_id=1, source_target_pairs={{0,1},{1,0},{2,3},{3,2},{4,5},{5,4},{6,7},{7,6},{8,9},{9,8},{10,11... | collective-permute-start | bytes 7077896 | tf_op jit(solution)/shard_map/ppermute | solution.py:103
  589.9 65.9 %collective-permute-start.47 = (bf16[4,96,768]{2,1,0:T(8,128)(2,1)}, bf16[4,96,768]{2,1,0:T(8,128)(2,1)}, u32[]{:S(2)}, u32[]{:S(2)}) collective-permute-start(bf16[4,96,768]{2,1,0:T(8,128)(2,1)} %select_bitcast_fusion.9), channel_id=1, source_target_pairs={{0,1},{1,0},{2,3},{3,2},{4,5},{5,4},{6,7},{7,6},{8,9},{9,8},{10,11... | collective-permute-start | bytes 1769480 | tf_op jit(solution)/shard_map/ppermute | solution.py:103
  602.3 21.0 %collective-permute-start.86 = (f32[1,768]{1,0:T(1,128)}, f32[1,768]{1,0:T(1,128)}, u32[]{:S(2)}, u32[]{:S(2)}) collective-permute-start(f32[1,768]{1,0:T(1,128)} %reshape.372), channel_id=1, source_target_pairs={{0,1},{1,0},{2,3},{3,2},{4,5},{5,4},{6,7},{7,6},{8,9},{9,8},{10,11... | collective-permute-start | bytes 9224 | tf_op jit(solution)/shard_map/ppermute | solution.py:103
  633.1 18.3 %collective-permute-start.89 = (f32[1,768]{1,0:T(1,128)S(1)}, f32[1,768]{1,0:T(1,128)S(1)}, u32[]{:S(2)}, u32[]{:S(2)}) collective-permute-start(f32[1,768]{1,0:T(1,128)S(1)} %add.671), channel_id=1, source_target_pairs={{0,2},{1,3},{2,4},{3,5},{4,6},{5,7},{6,0},{7,1},{8,10},{9,11},{10,... | collective-permute-start | bytes 9224 | tf_op jit(solution)/shard_map/ppermute | solution.py:104
  635.8 15.9 %collective-permute-start.90 = (f32[1,768]{1,0:T(1,128)S(1)}, f32[1,768]{1,0:T(1,128)S(1)}, u32[]{:S(2)}, u32[]{:S(2)}) collective-permute-start(f32[1,768]{1,0:T(1,128)S(1)} %add.671), channel_id=1, source_target_pairs={{0,4},{1,5},{2,6},{3,7},{4,0},{5,1},{6,2},{7,3},{8,12},{9,13},{10,... | collective-permute-start | bytes 9224 | tf_op jit(solution)/shard_map/ppermute | solution.py:104
  639.2 14.1 %collective-permute-start.91 = (f32[1,768]{1,0:T(1,128)S(1)}, f32[1,768]{1,0:T(1,128)S(1)}, u32[]{:S(2)}, u32[]{:S(2)}) collective-permute-start(f32[1,768]{1,0:T(1,128)S(1)} %add.671), channel_id=1, source_target_pairs={{0,6},{1,7},{2,0},{3,1},{4,2},{5,3},{6,4},{7,5},{8,14},{9,15},{10,... | collective-permute-start | bytes 9224 | tf_op jit(solution)/shard_map/ppermute | solution.py:104
  650.3 47.2 %collective-permute-start.69 = (bf16[4,384,768]{2,1,0:T(8,128)(2,1)}, bf16[4,384,768]{2,1,0:T(8,128)(2,1)S(1)}, u32[]{:S(2)}, u32[]{:S(2)}) collective-permute-start(bf16[4,384,768]{2,1,0:T(8,128)(2,1)} %select_bitcast_fusion), channel_id=1, source_target_pairs={{0,1},{1,0},{2,3},{3,2},{4,5},{5,4},{6,7},{7,6},{8,9},{9,8},{10,11... | collective-permute-start | bytes 7077896 | tf_op jit(solution)/shard_map/ppermute | solution.py:103
  651.4 35.7 %collective-permute-start.36 = (bf16[4,96,2304]{2,1,0:T(8,128)(2,1)}, bf16[4,96,2304]{2,1,0:T(8,128)(2,1)S(1)}, u32[]{:S(2)}, u32[]{:S(2)}) collective-permute-start(bf16[4,96,2304]{2,1,0:T(8,128)(2,1)} %select_bitcast_fusion.6), channel_id=1, source_target_pairs={{0,1},{1,0},{2,3},{3,2},{4,5},{5,4},{6,7},{7,6},{8,9},{9,8},{10,11... | collective-permute-start | bytes 5308424 | tf_op jit(solution)/shard_map/ppermute | solution.py:103
  684.3 18.4 %collective-permute-start.58 = (bf16[4,96,3072]{2,1,0:T(8,128)(2,1)S(1)}, bf16[4,96,3072]{2,1,0:T(8,128)(2,1)S(1)}, u32[]{:S(2)}, u32[]{:S(2)}) collective-permute-start(bf16[4,96,3072]{2,1,0:T(8,128)(2,1)S(1)} %copy-done.48), channel_id=1, source_target_pairs={{0,1},{1,0},{2,3},{3,2},{4,5},{5,4},{6,7},{7,6},{8,9},{9,8},{10,11... | collective-permute-start | bytes 7077896 | tf_op jit(solution)/shard_map/ppermute | solution.py:103
  697.2 10.7 %collective-permute-start.38 = (bf16[4,48,1152]{2,1,0:T(8,128)(2,1)S(1)}, bf16[4,48,1152]{2,1,0:T(8,128)(2,1)S(1)}, u32[]{:S(2)}, u32[]{:S(2)}) collective-permute-start(bf16[4,48,1152]{2,1,0:T(8,128)(2,1)S(1)} %pad_maximum_fusion.12), channel_id=1, source_target_pairs={{0,8},{8,0},{16,24},{24,16},{1,9},{9,1},{17,25},{25,17},{2,10},{10... | collective-permute-start | bytes 1327112 | tf_op jit(solution)/shard_map/ppermute | solution.py:100
  698.6 21.1 %collective-permute-start.70 = (bf16[2,192,384]{2,1,0:T(8,128)(2,1)S(1)}, bf16[2,192,384]{2,1,0:T(8,128)(2,1)S(1)}, u32[]{:S(2)}, u32[]{:S(2)}) collective-permute-start(bf16[2,192,384]{2,1,0:T(8,128)(2,1)S(1)} %get-tuple-element.378), channel_id=1, source_target_pairs={{0,16},{8,24},{16,0},{24,8},{1,17},{9,25},{17,1},{25,9},{2,18},{10... | collective-permute-start | bytes 884744 | tf_op jit(solution)/shard_map/ppermute | solution.py:101
  700.7 20.4 %collective-permute-start.72 = (bf16[2,192,384]{2,1,0:T(8,128)(2,1)S(1)}, bf16[2,192,384]{2,1,0:T(8,128)(2,1)S(1)}, u32[]{:S(2)}, u32[]{:S(2)}) collective-permute-start(bf16[2,192,384]{2,1,0:T(8,128)(2,1)S(1)} %get-tuple-element.380), channel_id=1, source_target_pairs={{0,8},{8,0},{16,24},{24,16},{1,9},{9,1},{17,25},{25,17},{2,10},{10... | collective-permute-start | bytes 884744 | tf_op jit(solution)/shard_map/ppermute | solution.py:100
  718.7 11.2 %collective-permute-start.44 = (bf16[48,1152]{1,0:T(8,128)(2,1)S(1)}, bf16[48,1152]{1,0:T(8,128)(2,1)S(1)}, u32[]{:S(2)}, u32[]{:S(2)}) collective-permute-start(bf16[48,1152]{1,0:T(8,128)(2,1)S(1)} %fusion.98), channel_id=1, source_target_pairs={{0,8},{8,0},{16,24},{24,16},{1,9},{9,1},{17,25},{25,17},{2,10},{10... | collective-permute-start | bytes 331784 | tf_op jit(solution)/shard_map/ppermute | solution.py:100
  719.7 10.8 %collective-permute-start.45 = (bf16[48,1152]{1,0:T(8,128)(2,1)S(1)}, bf16[48,1152]{1,0:T(8,128)(2,1)S(1)}, u32[]{:S(2)}, u32[]{:S(2)}) collective-permute-start(bf16[48,1152]{1,0:T(8,128)(2,1)S(1)} %fusion.98), channel_id=1, source_target_pairs={{0,16},{8,24},{16,0},{24,8},{1,17},{9,25},{17,1},{25,9},{2,18},{10... | collective-permute-start | bytes 331784 | tf_op jit(solution)/shard_map/ppermute | solution.py:101
  721.1 12.0 %collective-permute-start.46 = (bf16[48,1152]{1,0:T(8,128)(2,1)S(1)}, bf16[48,1152]{1,0:T(8,128)(2,1)S(1)}, u32[]{:S(2)}, u32[]{:S(2)}) collective-permute-start(bf16[48,1152]{1,0:T(8,128)(2,1)S(1)} %fusion.98), channel_id=1, source_target_pairs={{0,24},{8,16},{16,8},{24,0},{1,25},{9,17},{17,9},{25,1},{2,26},{10... | collective-permute-start | bytes 331784 | tf_op jit(solution)/shard_map/ppermute | solution.py:102
  725.1 16.3 %collective-permute-start.71 = (bf16[4,192,384]{2,1,0:T(8,128)(2,1)S(1)}, bf16[4,192,384]{2,1,0:T(8,128)(2,1)S(1)}, u32[]{:S(2)}, u32[]{:S(2)}) collective-permute-start(bf16[4,192,384]{2,1,0:T(8,128)(2,1)S(1)} %pad_maximum_fusion.9), channel_id=1, source_target_pairs={{0,8},{8,0},{16,24},{24,16},{1,9},{9,1},{17,25},{25,17},{2,10},{10... | collective-permute-start | bytes 1769480 | tf_op jit(solution)/shard_map/ppermute | solution.py:100
  727.5 15.1 %collective-permute-start.73 = (bf16[4,192,384]{2,1,0:T(8,128)(2,1)S(1)}, bf16[4,192,384]{2,1,0:T(8,128)(2,1)S(1)}, u32[]{:S(2)}, u32[]{:S(2)}) collective-permute-start(bf16[4,192,384]{2,1,0:T(8,128)(2,1)S(1)} %pad_maximum_fusion.10), channel_id=1, source_target_pairs={{0,16},{8,24},{16,0},{24,8},{1,17},{9,25},{17,1},{25,9},{2,18},{10... | collective-permute-start | bytes 1769480 | tf_op jit(solution)/shard_map/ppermute | solution.py:101
  729.9 17.8 %collective-permute-start.60 = (bf16[4,48,1536]{2,1,0:T(8,128)(2,1)S(1)}, bf16[4,48,1536]{2,1,0:T(8,128)(2,1)S(1)}, u32[]{:S(2)}, u32[]{:S(2)}) collective-permute-start(bf16[4,48,1536]{2,1,0:T(8,128)(2,1)S(1)} %pad_maximum_fusion.7), channel_id=1, source_target_pairs={{0,8},{8,0},{16,24},{24,16},{1,9},{9,1},{17,25},{25,17},{2,10},{10... | collective-permute-start | bytes 1769480 | tf_op jit(solution)/shard_map/ppermute | solution.py:100
  730.5 18.4 %collective-permute-start.62 = (bf16[4,48,1536]{2,1,0:T(8,128)(2,1)S(1)}, bf16[4,48,1536]{2,1,0:T(8,128)(2,1)S(1)}, u32[]{:S(2)}, u32[]{:S(2)}) collective-permute-start(bf16[4,48,1536]{2,1,0:T(8,128)(2,1)S(1)} %pad_maximum_fusion.8), channel_id=1, source_target_pairs={{0,16},{8,24},{16,0},{24,8},{1,17},{9,25},{17,1},{25,9},{2,18},{10... | collective-permute-start | bytes 1769480 | tf_op jit(solution)/shard_map/ppermute | solution.py:101
  743.0 11.3 %collective-permute-start.74 = (bf16[192,384]{1,0:T(8,128)(2,1)S(1)}, bf16[192,384]{1,0:T(8,128)(2,1)S(1)}, u32[]{:S(2)}, u32[]{:S(2)}) collective-permute-start(bf16[192,384]{1,0:T(8,128)(2,1)S(1)} %get-tuple-element.412), channel_id=1, source_target_pairs={{0,2},{1,3},{2,4},{3,5},{4,6},{5,7},{6,0},{7,1},{8,10},{9,11},{10,... | collective-permute-start | bytes 442376 | tf_op jit(solution)/shard_map/ppermute | solution.py:104
  743.3 15.3 %collective-permute-start.75 = (bf16[192,384]{1,0:T(8,128)(2,1)S(1)}, bf16[192,384]{1,0:T(8,128)(2,1)S(1)}, u32[]{:S(2)}, u32[]{:S(2)}) collective-permute-start(bf16[192,384]{1,0:T(8,128)(2,1)S(1)} %get-tuple-element.414), channel_id=1, source_target_pairs={{0,4},{1,5},{2,6},{3,7},{4,0},{5,1},{6,2},{7,3},{8,12},{9,13},{10,... | collective-permute-start | bytes 442376 | tf_op jit(solution)/shard_map/ppermute | solution.py:104
  746.5 12.2 %collective-permute-start.76 = (bf16[192,384]{1,0:T(8,128)(2,1)S(1)}, bf16[192,384]{1,0:T(8,128)(2,1)S(1)}, u32[]{:S(2)}, u32[]{:S(2)}) collective-permute-start(bf16[192,384]{1,0:T(8,128)(2,1)S(1)} %get-tuple-element.413), channel_id=1, source_target_pairs={{0,6},{1,7},{2,0},{3,1},{4,2},{5,3},{6,4},{7,5},{8,14},{9,15},{10,... | collective-permute-start | bytes 442376 | tf_op jit(solution)/shard_map/ppermute | solution.py:104
  749.6 13.7 %collective-permute-start.64 = (bf16[48,1536]{1,0:T(8,128)(2,1)S(1)}, bf16[48,1536]{1,0:T(8,128)(2,1)S(1)}, u32[]{:S(2)}, u32[]{:S(2)}) collective-permute-start(bf16[48,1536]{1,0:T(8,128)(2,1)S(1)} %get-tuple-element.421), channel_id=1, source_target_pairs={{0,4},{1,5},{2,6},{3,7},{4,0},{5,1},{6,2},{7,3},{8,12},{9,13},{10,... | collective-permute-start | bytes 442376 | tf_op jit(solution)/shard_map/ppermute | solution.py:104
  783.9 11.4 %collective-permute-start.97 = (f32[1,4]{1,0:T(1,128)S(1)}, f32[1,4]{1,0:T(1,128)S(1)}, u32[]{:S(2)}, u32[]{:S(2)}) collective-permute-start(f32[1,4]{1,0:T(1,128)S(1)} %fusion.167), channel_id=1, source_target_pairs={{0,2},{1,3},{2,4},{3,5},{4,6},{5,7},{6,0},{7,1},{8,10},{9,11},{10,... | collective-permute-start | bytes 56 | tf_op jit(solution)/shard_map/ppermute | solution.py:104
  (173 other events, 3740.0 us)

commit v2 on v0

v2 whole, which is shorter than its diff:
```python
from functools import partial

import jax
import jax.numpy as jnp
from jax import lax
from jax.experimental import pallas as pl
from jax.experimental.pallas import tpu as pltpu
from jax.sharding import PartitionSpec as P

H = 12
HD = 64
STEP = 10
QT = 256
KT = 128
PAIRS = 3
VARIANTS = (2, 3, 4, 5, 7, 8)
norm_eps = 1e-06
bf = jnp.bfloat16
f32 = jnp.float32


def nt(a, b):
    return lax.dot_general(a, b, (((1,), (1,)), ((), ())), preferred_element_type=f32)


def nn(a, b):
    return lax.dot_general(a, b, (((1,), (0,)), ((), ())), preferred_element_type=f32)


def rnd(v):
    return v.astype(bf)


def up(v):
    return v.astype(f32)


def params(mib=48):
    return pltpu.CompilerParams(vmem_limit_bytes=mib << 20)


def cost(flops, moved):
    return pl.CostEstimate(flops=int(flops), bytes_accessed=int(moved), transcendentals=0)


def shaped(shape, kind):
    return jax.ShapeDtypeStruct(shape, kind)


def row_norm(v):
    centre = jnp.mean(v, axis=-1, keepdims=True)
    centred = v - centre
    spread = jnp.mean(centred * centred, axis=-1, keepdims=True)
    scale = lax.rsqrt(spread + norm_eps)
    return centred * scale, scale


def first_kernel(tok_ref, vec_ref, freq_ref, grid_ref, n_ref, nt_ref, cos_ref, sin_ref):
    w = tok_ref.shape[1]
    hat, scale = row_norm(up(tok_ref[...]))
    normed = hat * vec_ref[:, :w] + vec_ref[:, w : 2 * w]
    n_ref[...] = rnd(normed)
    nt_ref[...] = rnd(normed.T)
    g = grid_ref[...]
    angle = g[:, 0:1] * freq_ref[0:1, :] + g[:, 1:2] * freq_ref[1:2, :]
    lane = lax.broadcasted_iota(jnp.int32, (1, w), 1)
    cos_ref[...] = jnp.cos(angle)
    s = jnp.sin(angle)
    sin_ref[...] = jnp.where(lane & 63 < 32, -s, s)


def first(tokens, vec, freq, grid_t):
    n, w = tokens.shape
    rows = lambda: pl.BlockSpec((QT, w), lambda i: (i, 0))
    whole = lambda a: pl.BlockSpec(a.shape, lambda i: (0, 0))
    return pl.pallas_call(
        first_kernel,
        name="first",
        grid=(n // QT,),
        in_specs=[rows(), whole(vec), whole(freq), pl.BlockSpec((QT, 2), lambda i: (i, 0))],
        out_specs=[rows(), pl.BlockSpec((w, QT), lambda i: (0, i)), rows(), rows()],
        out_shape=[shaped((n, w), bf), shaped((w, n), bf), shaped((n, w), f32), shaped((n, w), f32)],
        compiler_params=params(),
        cost_estimate=cost(1e10, 1e7),
    )(tokens, vec, freq, grid_t)


def swap(v):
    w = v.shape[1]
    lane = lax.broadcasted_iota(jnp.int32, (1, w), 1)
    return jnp.where(lane & 63 < 32, pltpu.roll(v, w - 32, 1), pltpu.roll(v, 32, 1))


def project_kernel(n_ref, w_ref, b_ref, cos_ref, sin_ref, o_ref):
    j = pl.program_id(0)
    u = nn(n_ref[...], w_ref[...]) + b_ref[...]

    @pl.when(j < 6)
    def _():
        turned = u * cos_ref[...] + swap(u) * sin_ref[...]
        o_ref[...] = rnd(turned * jnp.where(j < 3, 0.125, 1.0))

    @pl.when(j >= 6)
    def _():
        o_ref[...] = rnd(u)


def project(normed, weight, vec, cos, sin):
    n, w = normed.shape
    return pl.pallas_call(
        project_kernel,
        name="project",
        grid=(9,),
        in_specs=[
            pl.BlockSpec((n, w), lambda j: (0, 0)),
            pl.BlockSpec((w, 256), lambda j: (0, j)),
            pl.BlockSpec((1, 256), lambda j: (0, 12 + j)),
            pl.BlockSpec((n, 256), lambda j: (0, jnp.where(j < 6, j % 3, 2))),
            pl.BlockSpec((n, 256), lambda j: (0, jnp.where(j < 6, j % 3, 2))),
        ],
        out_specs=pl.BlockSpec((n, 256), lambda j: (0, j)),
        out_shape=shaped((n, 3 * w), bf),
        compiler_params=params(),
        cost_estimate=cost(8e9, 1e7),
    )(normed, weight, vec, cos, sin)


def tables(ids):
    n = ids.shape[0]
    lane = jnp.arange(128) & 63
    one = (ids[:, None] + 1 == lane[None]).astype(f32)
    small = (lane < 8)[None]
    aug_q = rnd(jnp.where(small, one, 0.0))
    aug_k = rnd(jnp.where(small, (one - 1.0) * 1e30, jnp.where((lane < 11)[None], 1.0, 0.0)))
    tiles = n // QT
    hit = (ids.reshape(tiles, QT, 1) == ids[None, None, :]).any(1)
    pos = jnp.arange(n)[None]
    lo = jnp.min(jnp.where(hit, pos, n), 1) // KT
    hi = jnp.max(jnp.where(hit, pos, -1), 1) // KT + 1
    need = hi - lo
    width = jnp.full_like(need, VARIANTS[-1])
    for v in VARIANTS[::-1]:
        width = jnp.where(need <= v, v, width)
    start = jnp.minimum(lo, n // KT - width)
    return aug_q, aug_k, jnp.stack([start, width]).astype(jnp.int32)


def low_lanes():
    return lax.broadcasted_iota(jnp.int32, (1, 128), 1) < 64


def attend_kernel(rng, q_ref, k_ref, v_ref, aq_ref, ak_ref, mix_ref, mixt_ref, lb_ref, vt):
    i = pl.program_id(1)
    n = k_ref.shape[0]
    start = rng[0, i]
    width = rng[1, i]
    low = low_lanes()

    @pl.when(i == 0)
    def _():
        one = jnp.ones((16, n), bf)
        for p in range(PAIRS):
            t = v_ref[:, 128 * p : 128 * p + 128].T
            for h in (0, 1):
                vt[2 * p + h, :64, :] = t[64 * h : 64 * h + 64]
                vt[2 * p + h, 64:, :] = one

    aq = aq_ref[...]
    for W in VARIANTS:

        @pl.when(width == W)
        def _():
            at = pl.ds(pl.multiple_of(start * KT, KT), W * KT)
            ak = ak_ref[at, :]
            scores = []
            for p in range(PAIRS):
                c = slice(128 * p, 128 * p + 128)
                q = q_ref[:, c]
                k = k_ref[at, c]
                scores.append(nt(jnp.where(low, k, ak), jnp.where(low, q, aq)))
                scores.append(nt(jnp.where(low, ak, k), jnp.where(low, aq, q)))
            for p in range(PAIRS):
                c = slice(128 * p, 128 * p + 128)
                outs = []
                for h in (0, 1):
                    s = scores[2 * p + h]
                    m = jnp.max(s, axis=0, keepdims=True)
                    e = rnd(jnp.exp(s - m))
                    o = nn(vt[2 * p + h, :, at], e)
                    t = o[64:65]
                    outs.append(o[:64] * (1.0 / t))
                    lb_ref[p, h : h + 1, :] = m + jnp.log(t)
                both = jnp.concatenate(outs, 0)
                mix_ref[:, c] = rnd(both.T)
                mixt_ref[c, :] = rnd(both)


def attend(qkv, aug_q, aug_k, rng):
    n, w3 = qkv.shape
    w = w3 // 3
    L = 128 * PAIRS
    g = w // L
    spec = pltpu.PrefetchScalarGridSpec(
        num_scalar_prefetch=1,
        grid=(g, n // QT),
        in_specs=[
            pl.BlockSpec((QT, L), lambda p, i, r: (i, p)),
            pl.BlockSpec((n, L), lambda p, i, r: (0, g + p)),
            pl.BlockSpec((n, L), lambda p, i, r: (0, 2 * g + p)),
            pl.BlockSpec((QT, 128), lambda p, i, r: (i, 0)),
            pl.BlockSpec((n, 128), lambda p, i, r: (0, 0)),
        ],
        out_specs=[
            pl.BlockSpec((QT, L), lambda p, i, r: (i, p)),
            pl.BlockSpec((L, QT), lambda p, i, r: (p, i)),
            pl.BlockSpec((PAIRS, 8, QT), lambda p, i, r: (p, 0, i)),
        ],
        scratch_shapes=[pltpu.VMEM((2 * PAIRS, 80, n), bf)],
    )
    return pl.pallas_call(
        attend_kernel,
        name="attend",
        grid_spec=spec,
        out_shape=[shaped((n, w), bf), shaped((w, n), bf), shaped((w // 128, 8, n), f32)],
        compiler_params=params(),
        cost_estimate=cost(2.3e10, 1e7),
    )(rng, qkv, qkv, qkv, aug_q, aug_k)


def fill(aug, x):
    lane = lax.broadcasted_iota(jnp.int32, (1, 128), 1) & 63
    a = rnd(x)
    r = x - up(a)
    b = rnd(r)
    c = rnd(r - up(b))
    return jnp.where(lane == 8, a, jnp.where(lane == 9, b, jnp.where(lane == 10, c, aug)))


def attend_back_kernel(
    rng, q_ref, k_ref, v_ref, g_ref, mix_ref, lb_ref, aq_ref, ak_ref,
    dq_ref, dk_ref, dv_ref, dk_acc, dv_acc,
):
    i = pl.program_id(0)
    start = rng[0, i]
    width = rng[1, i]

    @pl.when(i == 0)
    def _():
        dk_acc[...] = jnp.zeros_like(dk_acc)
        dv_acc[...] = jnp.zeros_like(dv_acc)

    low = low_lanes()
    aq0 = aq_ref[...]
    zero = jnp.zeros((1, 128), bf)
    held = []
    for p in range(PAIRS):
        c = slice(128 * p, 128 * p + 128)
        q = q_ref[:, c]
        g = g_ref[:, c]
        prod = up(g) * up(mix_ref[:, c])
        even = jnp.sum(jnp.where(low, prod, 0.0), axis=1, keepdims=True)
        odd = jnp.sum(jnp.where(low, 0.0, prod), axis=1, keepdims=True)
        lt = lb_ref[p].T
        aq = fill(aq0, -jnp.where(low, lt[:, 1:2], lt[:, 0:1]))
        ag = fill(zero, -jnp.where(low, odd, even))
        held.append(
            (
                (jnp.where(low, q, aq), jnp.where(low, aq, q)),
                (jnp.where(low, g, ag), jnp.where(low, ag, g)),
                q.T,
                g.T,
            )
        )
    for W in VARIANTS:

        @pl.when(width == W)
        def _():
            at = pl.ds(pl.multiple_of(start * KT, KT), W * KT)
            ak = ak_ref[at, :]
            for p in range(PAIRS):
                c = slice(128 * p, 128 * p + 128)
                qs, gs, qt, gt = held[p]
                k = k_ref[at, c]
                v = v_ref[at, c]
                one = jnp.ones_like(v)
                ks = (jnp.where(low, k, ak), jnp.where(low, ak, k))
                vs = (jnp.where(low, v, one), jnp.where(low, one, v))
                dqs = []
                for h in (0, 1):
                    e = jnp.exp(nt(qs[h], ks[h]))
                    ds = rnd(e * nt(gs[h], vs[h]))
                    e = rnd(e)
                    half = slice(64 * h, 64 * h + 64)
                    to = slice(128 * p + 64 * h, 128 * p + 64 * h + 64)
                    dqs.append(nn(ds, k))
                    dk_acc[to, at] += nn(qt[half], ds)
                    dv_acc[to, at] += nn(gt[half], e)
                dq_ref[:, c] = jnp.where(low, dqs[0], dqs[1]) * 0.125

    @pl.when(i == pl.num_programs(0) - 1)
    def _():
        dk_ref[...] = dk_acc[...].T
        dv_ref[...] = rnd(dv_acc[...].T)


def attend_back(part, qkv, g_mix, mix, lb, aug_q, aug_k, rng):
    n, w3 = qkv.shape
    L = 128 * PAIRS
    g = w3 // 3 // L
    spec = pltpu.PrefetchScalarGridSpec(
        num_scalar_prefetch=1,
        grid=(n // QT,),
        in_specs=[
            pl.BlockSpec((QT, L), lambda i, r: (i, part)),
            pl.BlockSpec((n, L), lambda i, r: (0, g + part)),
            pl.BlockSpec((n, L), lambda i, r: (0, 2 * g + part)),
            pl.BlockSpec((QT, L), lambda i, r: (i, part)),
            pl.BlockSpec((QT, L), lambda i, r: (i, part)),
            pl.BlockSpec((PAIRS, 8, QT), lambda i, r: (part, 0, i)),
            pl.BlockSpec((QT, 128), lambda i, r: (i, 0)),
            pl.BlockSpec((n, 128), lambda i, r: (0, 0)),
        ],
        out_specs=[
            pl.BlockSpec((QT, L), lambda i, r: (i, 0)),
            pl.BlockSpec((n, L), lambda i, r: (0, 0)),
            pl.BlockSpec((n, L), lambda i, r: (0, 0)),
        ],
        scratch_shapes=[pltpu.VMEM((L, n), f32), pltpu.VMEM((L, n), f32)],
    )
    return pl.pallas_call(
        attend_back_kernel,
        name="attend_back",
        grid_spec=spec,
        out_shape=[shaped((n, L), f32), shaped((n, L), f32), shaped((n, L), bf)],
        compiler_params=params(),
        cost_estimate=cost(2.2e10, 1e7),
    )(rng, qkv, qkv, qkv, g_mix, mix, lb, aug_q, aug_k)


def branch_kernel(tok_ref, mix_ref, w_ref, vec_ref, res_ref, n_ref, nt_ref):
    w = tok_ref.shape[1]
    resid = up(tok_ref[...]) + nn(mix_ref[...], w_ref[...]) + vec_ref[:, 7 * w : 8 * w]
    res_ref[...] = resid
    hat, scale = row_norm(resid)
    normed = hat * vec_ref[:, 2 * w : 3 * w] + vec_ref[:, 3 * w : 4 * w]
    n_ref[...] = rnd(normed)
    nt_ref[...] = rnd(normed.T)


def branch(tokens, mix, weight, vec):
    n, w = tokens.shape
    rows = lambda: pl.BlockSpec((QT, w), lambda i: (i, 0))
    whole = lambda a: pl.BlockSpec(a.shape, lambda i: (0, 0))
    return pl.pallas_call(
        branch_kernel,
        name="branch",
        grid=(n // QT,),
        in_specs=[rows(), rows(), whole(weight), whole(vec)],
        out_specs=[rows(), rows(), pl.BlockSpec((w, QT), lambda i: (0, i))],
        out_shape=[shaped((n, w), f32), shaped((n, w), bf), shaped((w, n), bf)],
        compiler_params=params(),
        cost_estimate=cost(4e9, 1e7),
    )(tokens, mix, weight, vec)


def gelu_parts(x):
    z = jnp.abs(x)
    e = jnp.exp(x * x * -0.5)
    t = 1.0 / (1.0 + (0.3275911 * 0.7071067811865476) * z)
    poly = t * (
        0.5 * 0.254829592
        + t
        * (
            0.5 * -0.284496736
            + t * (0.5 * 1.421413741 + t * (0.5 * -1.453152027 + t * (0.5 * 1.061405429)))
        )
    )
    tail = poly * e
    cdf = jnp.where(x < 0.0, tail, 1.0 - tail)
    return x * cdf, cdf + x * (e * 0.3989422804014327)


def hidden_kernel(n_ref, w_ref, b_ref, a_ref, at_ref, d_ref):
    x = nn(n_ref[...], w_ref[...]) + b_ref[...]
    active, slope = gelu_parts(x)
    active = rnd(active)
    a_ref[...] = active
    at_ref[...] = active.T
    d_ref[...] = rnd(slope)


def hidden_units(normed, weight, vec):
    n, w = normed.shape
    ff = weight.shape[1]
    B = 256
    off = 8 * w // B
    return pl.pallas_call(
        hidden_kernel,
        name="hidden",
        grid=(ff // B,),
        in_specs=[
            pl.BlockSpec((n, w), lambda j: (0, 0)),
            pl.BlockSpec((w, B), lambda j: (0, j)),
            pl.BlockSpec((1, B), lambda j: (0, off + j)),
        ],
        out_specs=[
            pl.BlockSpec((n, B), lambda j: (0, j)),
            pl.BlockSpec((B, n), lambda j: (j, 0)),
            pl.BlockSpec((n, B), lambda j: (0, j)),
        ],
        out_shape=[shaped((n, ff), bf), shaped((ff, n), bf), shaped((n, ff), bf)],
        compiler_params=params(),
        cost_estimate=cost(1.5e10, 1e7),
    )(normed, weight, vec)


def last_kernel(a_ref, w_ref, res_ref, b_ref, o_ref):
    o_ref[...] = rnd(res_ref[...] + nn(a_ref[...], w_ref[...]) + b_ref[...])


def last(active, weight, resid, vec):
    n, ff = active.shape
    w = resid.shape[1]
    off = (8 * w + ff) // w
    return pl.pallas_call(
        last_kernel,
        name="last",
        grid=(n // QT,),
        in_specs=[
            pl.BlockSpec((QT, ff), lambda i: (i, 0)),
            pl.BlockSpec((ff, w), lambda i: (0, 0)),
            pl.BlockSpec((QT, w), lambda i: (i, 0)),
            pl.BlockSpec((1, w), lambda i: (0, off)),
        ],
        out_specs=pl.BlockSpec((QT, w), lambda i: (i, 0)),
        out_shape=shaped((n, w), bf),
        compiler_params=params(),
        cost_estimate=cost(6e9, 1e7),
    )(active, weight, resid, vec)


def hidden_back_kernel(g_ref, w_ref, d_ref, gh_ref, sum_ref):
    gh = rnd(nt(g_ref[...], w_ref[...]) * up(d_ref[...]))
    gh_ref[...] = gh
    sum_ref[...] = jnp.sum(up(gh), axis=0, keepdims=True)


def hidden_back(given, weight, slope):
    n, w = given.shape
    ff = weight.shape[0]
    B = 512
    return pl.pallas_call(
        hidden_back_kernel,
        name="hidden_back",
        grid=(ff // B,),
        in_specs=[
            pl.BlockSpec((n, w), lambda j: (0, 0)),
            pl.BlockSpec((B, w), lambda j: (j, 0)),
            pl.BlockSpec((n, B), lambda j: (0, j)),
        ],
        out_specs=[pl.BlockSpec((n, B), lambda j: (0, j)), pl.BlockSpec((1, B), lambda j: (0, j))],
        out_shape=[shaped((n, ff), bf), shaped((1, ff), f32)],
        compiler_params=params(),
        cost_estimate=cost(8e9, 1e7),
    )(given, weight, slope)


def norm_back(grad, hat, scale, gain):
    d = grad * gain
    a = jnp.mean(d, axis=-1, keepdims=True)
    b = jnp.mean(d * hat, axis=-1, keepdims=True)
    return (d - a - hat * b) * scale


def second_back_kernel(gh_ref, w_ref, res_ref, cot_ref, vec_ref, wo_ref, gr_ref, gb_ref, gm_ref, sum_ref):
    i = pl.program_id(0)
    w = res_ref.shape[1]
    grad = nt(gh_ref[...], w_ref[...])
    hat, scale = row_norm(res_ref[...])
    total = up(cot_ref[...]) + norm_back(grad, hat, scale, vec_ref[:, 2 * w : 3 * w])
    gr_ref[...] = total
    low = rnd(total)
    gb_ref[...] = low
    gm_ref[...] = rnd(nt(low, wo_ref[...]))
    sums = jnp.concatenate(
        [
            jnp.sum(grad * hat, axis=0, keepdims=True),
            jnp.sum(grad, axis=0, keepdims=True),
            jnp.sum(up(low), axis=0, keepdims=True),
        ],
        axis=0,
    )

    @pl.when(i == 0)
    def _():
        sum_ref[...] = jnp.zeros_like(sum_ref)

    sum_ref[0:3, :] += sums


def second_back(gh, weight, resid, given, vec, out_w):
    n, ff = gh.shape
    w = resid.shape[1]
    rows = lambda c: pl.BlockSpec((QT, c), lambda i: (i, 0))
    whole = lambda a: pl.BlockSpec(a.shape, lambda i: (0, 0))
    return pl.pallas_call(
        second_back_kernel,
        name="second_back",
        grid=(n // QT,),
        in_specs=[rows(ff), whole(weight), rows(w), rows(w), whole(vec), whole(out_w)],
        out_specs=[rows(w), rows(w), rows(w), pl.BlockSpec((8, w), lambda i: (0, 0))],
        out_shape=[shaped((n, w), f32), shaped((n, w), bf), shaped((n, w), bf), shaped((8, w), f32)],
        compiler_params=params(),
        cost_estimate=cost(9e9, 1e7),
    )(gh, weight, resid, given, vec, out_w)


def outer_kernel(sel, x_ref, y_ref, o_ref):
    z, one, r, n = x_ref.shape
    got = nn(x_ref[...].reshape(z * r, n), y_ref[...])
    o_ref[...] = rnd(got).reshape(o_ref.shape)


def outer(x_t, y, sel, groups, share):
    rows, n = x_t.shape
    c = y.shape[1]
    r = rows // (groups * share)
    B = 256 if rows > 2 * c else 512 if c % 512 == 0 else 384 if c % 384 == 0 else 256
    spec = pltpu.PrefetchScalarGridSpec(
        num_scalar_prefetch=1,
        grid=(c // B,),
        in_specs=[
            pl.BlockSpec((groups, 1, r, n), lambda j, s: (0, s[0], 0, 0)),
            pl.BlockSpec((n, B), lambda j, s: (0, j)),
        ],
        out_specs=pl.BlockSpec((groups, r, B), lambda j, s: (0, 0, j)),
    )
    return pl.pallas_call(
        outer_kernel,
        name="outer",
        grid_spec=spec,
        out_shape=shaped((groups, r, c), bf),
        compiler_params=params(),
        cost_estimate=cost(4 * groups * r * c * n, 1e7),
    )(sel, x_t.reshape(groups, share, r, n), y)


def turn_back_kernel(
    dq_ref, dk_ref, dv_ref, q_ref, k_ref, cos_ref, sin_ref, grid_ref, gp_ref, b_ref, f_ref
):
    i = pl.program_id(0)
    w = cos_ref.shape[1]
    cos = cos_ref[...]
    sin = sin_ref[...]
    dq = dq_ref[...]
    dk = dk_ref[...]
    gv = dv_ref[...]
    sq = swap(dq)
    sk = swap(dk)
    t = sq * (up(q_ref[...]) * 8.0) + sk * up(k_ref[...])
    g = grid_ref[...]
    gq = rnd(dq * cos - sq * sin)
    gk = rnd(dk * cos - sk * sin)
    gp_ref[:, :w] = gq
    gp_ref[:, w : 2 * w] = gk
    gp_ref[:, 2 * w :] = gv
    add = lambda v: jnp.sum(v, axis=0, keepdims=True)

    @pl.when(i == 0)
    def _():
        b_ref[...] = jnp.zeros_like(b_ref)
        f_ref[...] = jnp.zeros_like(f_ref)

    b_ref[0:3, :] += jnp.concatenate([add(up(gq)), add(up(gk)), add(up(gv))], axis=0)
    f_ref[0:2, :] += jnp.concatenate([add(t * g[:, 0:1]), add(t * g[:, 1:2])], axis=0)


def turn_back(part, dq, dk, dv, qkv, cos, sin, grid_t):
    n, L = dq.shape
    g = qkv.shape[1] // 3 // L
    rows = lambda c, j=0: pl.BlockSpec((QT, c), lambda i: (i, j))
    fixed = lambda: pl.BlockSpec((8, L), lambda i: (0, 0))
    return pl.pallas_call(
        turn_back_kernel,
        name="turn_back",
        grid=(n // QT,),
        in_specs=[rows(L), rows(L), rows(L), rows(L, part), rows(L, g + part)]
        + [rows(L, part), rows(L, part), pl.BlockSpec((QT, 2), lambda i: (i, 0))],
        out_specs=[rows(3 * L), fixed(), fixed()],
        out_shape=[shaped((n, 3 * L), bf), shaped((8, L), f32), shaped((8, L), f32)],
        compiler_params=params(),
        cost_estimate=cost(4e9, 1e7),
    )(dq, dk, dv, qkv, qkv, cos, sin, grid_t)


def first_back_kernel(*refs):
    gp_refs = refs[:-6]
    w_ref, tok_ref, gr_ref, vec_ref, o_ref, sum_ref = refs[-6:]
    i = pl.program_id(0)
    w = tok_ref.shape[1]
    L = w // len(gp_refs)
    gp = [r[:, s * L : (s + 1) * L] for s in range(3) for r in gp_refs]
    grad = nt(jnp.concatenate(gp, axis=1), w_ref[...])
    hat, scale = row_norm(up(tok_ref[...]))
    o_ref[...] = rnd(gr_ref[...] + norm_back(grad, hat, scale, vec_ref[:, :w]))
    sums = jnp.concatenate(
        [jnp.sum(grad * hat, axis=0, keepdims=True), jnp.sum(grad, axis=0, keepdims=True)], axis=0
    )

    @pl.when(i == 0)
    def _():
        sum_ref[...] = jnp.zeros_like(sum_ref)

    sum_ref[0:2, :] += sums


def first_back(gps, weight, tokens, grad_resid, vec):
    n, w = tokens.shape
    rows = lambda c: pl.BlockSpec((QT, c), lambda i: (i, 0))
    whole = lambda a: pl.BlockSpec(a.shape, lambda i: (0, 0))
    return pl.pallas_call(
        first_back_kernel,
        name="first_back",
        grid=(n // QT,),
        in_specs=[rows(g.shape[1]) for g in gps] + [whole(weight), rows(w), rows(w), whole(vec)],
        out_specs=[rows(w), pl.BlockSpec((8, w), lambda i: (0, 0))],
        out_shape=[shaped((n, w), bf), shaped((8, w), f32)],
        compiler_params=params(),
        cost_estimate=cost(7e9, 1e7),
    )(*gps, weight, tokens, grad_resid, vec)


def over_dp(v, k):
    return lax.ppermute(v, "dp", [(i, i ^ k) for i in range(4)])


def over_core(v):
    return lax.ppermute(v, "fsdp", [(i, i ^ 1) for i in range(8)])


def over_z(v, k):
    return lax.ppermute(v, "fsdp", [(i, i ^ (2 * k)) for i in range(8)])


def along_z(v, s):
    return lax.ppermute(v, "fsdp", [(i, (i + 2 * s) % 8) for i in range(8)])


def tie(*values):
    return lax.optimization_barrier(values)


def place():
    d = lax.axis_index("dp")
    f = lax.axis_index("fsdp")
    return d, f // 2, f % 2


def quarter(shard):
    d, z, c = place()
    r, cols = shard.shape
    return lax.dynamic_slice(shard, (d * (r // 4), 0), (r // 4, cols))


def spread_z(part):
    return jnp.stack([part] + [along_z(part, s) for s in (1, 2, 3)])


def spread_dp(column):
    return [column] + [over_dp(column, k) for k in (1, 2, 3)]


def arrange_kernel(at, *refs):
    out = refs[-1]
    for side in (0, 1):
        for k in range(4):
            for s in range(4):
                to = ((lax.rem(at[1] + 4 - s, 4) * 2 + lax.bitwise_xor(at[2], side)) * 4) + lax.bitwise_xor(at[0], k)
                out[to] = refs[side * 4 + k][s]


def arrange(own, other):
    d, z, c = place()
    at = jnp.stack([d, z, c]).astype(jnp.int32)
    r, cols = own[0].shape[1:]
    B = cols // 3
    spec = pltpu.PrefetchScalarGridSpec(
        num_scalar_prefetch=1,
        grid=(3,),
        in_specs=[pl.BlockSpec((4, r, B), lambda j, a: (0, 0, j))] * 8,
        out_specs=pl.BlockSpec((32, r, B), lambda j, a: (0, 0, j)),
    )
    out = pl.pallas_call(
        arrange_kernel,
        name="arrange",
        grid_spec=spec,
        out_shape=shaped((32, r, cols), bf),
        compiler_params=params(),
        cost_estimate=cost(1e6, 4 * 32 * r * cols),
    )(at, *own, *other)
    return out.reshape(32 * r, cols)


def at_index(v, axis, k):
    return lax.dynamic_index_in_dim(v, k, axis, keepdims=False)


def fold_core(mine, other):
    d, z, c = place()
    groups, r, cols = mine.shape
    both = rnd(up(mine) + up(other)).reshape(groups, 4, r // 4, cols)
    return [at_index(both, 1, lax.bitwise_xor(d, k)) for k in range(4)]


def fold_dp(pieces):
    own, got = pieces
    d, z, c = place()
    total = up(own)
    for g in got:
        total = total + up(g)
    total = rnd(total)
    return [at_index(total, 0, lax.rem(z + s, 4)) for s in range(4)]


def fold_z(own, got):
    total = up(own)
    for g in got:
        total = total + up(g)
    return rnd(total)


def share(own, got):
    d, z, c = place()
    all_of = [own] + got
    rows = []
    for j in range(4):
        rel = lax.bitwise_xor(d, j)
        v = all_of[3]
        for k in (2, 1, 0):
            v = jnp.where(rel == k, all_of[k], v)
        rows.append(v)
    return up(jnp.concatenate(rows, 0))


def doubled(v, other, bit):
    return jnp.concatenate([jnp.where(bit == 0, v, other), jnp.where(bit == 0, other, v)], 0)


def gather_vector(shard):
    d, z, c = place()
    v = shard.reshape(1, -1)
    v = doubled(v, over_core(v), c)
    v = doubled(v, over_z(v, 1), z % 2)
    v = doubled(v, over_z(v, 2), z // 2)
    return v.reshape(-1)


def sum_dp(v):
    v = v + over_dp(v, 1)
    return v + over_dp(v, 2)


def sum_fsdp(v):
    v = v + over_core(v)
    v = v + over_z(v, 1)
    return v + over_z(v, 2)


def sum_dp_low(v):
    v = rnd(up(v) + up(over_dp(v, 1)))
    return rnd(up(v) + up(over_dp(v, 2)))


def adam_terms(grad, first, second, master, decay):
    first_new = 0.9 * first + 0.1 * grad
    second_new = 0.999 * second + 0.001 * grad * grad
    first_hat = first_new / (1.0 - 0.9**STEP)
    second_hat = second_new / (1.0 - 0.999**STEP)
    update = first_hat / (jnp.sqrt(second_hat) + 1e-06) + decay * master
    return (first_new, second_new, update)


def body(fast, tokens, cotangent, image_ids, patch_grid, *state):
    masters, vectors = state[:4], state[4]
    firsts, vector_first = state[5:9], state[9]
    seconds, vector_second = state[10:14], state[14]
    n, w = tokens.shape
    heads = w // HD
    count = w // 128 // PAIRS
    low = [rnd(m) for m in masters]
    gather = lambda v: lax.all_gather(v, "fsdp", axis=0, tiled=True)
    scatter = lambda v: lax.psum_scatter(v, "fsdp", scatter_dimension=0, tiled=True)
    whole = jnp.zeros((1,), jnp.int32)
    d, z, c = place()
    mine = jnp.stack([c]).astype(jnp.int32)

    if fast:
        qkv_column = spread_z(quarter(low[0]))
        packed = gather_vector(rnd(vectors))
        full_out = gather(low[1])
        up_part, _ = tie(quarter(low[2]), qkv_column)
        up_column = spread_z(up_part)
        down_part, _ = tie(low[3], full_out)
        full_down = gather(down_part)
        qkv_own = spread_dp(qkv_column)
    else:
        packed = gather(rnd(vectors))
        full_qkv, full_out, full_up, full_down = [gather(v) for v in low]
    vec = up(packed).reshape(1, -1)
    freq = vec[0, -w:].reshape(2, heads, 1, HD // 2)
    freq = jnp.broadcast_to(freq, (2, heads, 2, HD // 2)).reshape(2, w)
    grid_t = up(patch_grid.T)
    given = jnp.where((image_ids >= 0)[:, None], cotangent, jnp.zeros_like(cotangent))
    grad_bias_down = jnp.sum(up(given), axis=0)
    weight_local = jnp.stack([jnp.sum(m * m) for m in masters])
    aug_q, aug_k, rng = tables(image_ids)

    normed, normed_t, cos, sin = first(tokens, vec, freq, grid_t)
    if fast:
        normed, *qkv_own = tie(normed, *qkv_own)
        qkv_other = [over_core(v) for v in qkv_own]
        full_qkv = arrange(qkv_own, qkv_other)
        up_column, full_qkv = tie(up_column, full_qkv)
        up_own = spread_dp(up_column)
    qkv = project(normed, full_qkv, vec, cos, sin)
    mix, mix_t, lb = attend(qkv, aug_q, aug_k, rng)
    if fast:
        mix, *up_own = tie(mix, *up_own)
        up_other = [over_core(v) for v in up_own]
    resid, normed_two, normed_two_t = branch(tokens, mix, full_out, vec)
    if fast:
        full_up = arrange(up_own, up_other)
        normed_two, full_down = tie(normed_two, full_down)
    active, active_t, slope = hidden_units(normed_two, full_up, vec)
    if fast:
        theirs = outer(active_t, given, 1 - mine, 4, 2)
        down_sent = over_core(theirs)
        down_mine = outer(active_t, given, mine, 4, 2)
        down_pieces = fold_core(down_mine, down_sent)
        active, slope, *down_pieces = tie(active, slope, *down_pieces)
        down_got = [over_dp(v, k) for k, v in zip((1, 2, 3), down_pieces[1:])]
    else:
        down_full = outer(active_t, given, whole, 1, 1)[0]
    output = last(active, full_down, resid, vec)
    grad_hidden, grad_bias_up = hidden_back(given, full_down, slope)
    if fast:
        output, grad_hidden, *down_got = tie(output, grad_hidden, *down_got)
        down_z = fold_dp((down_pieces[0], down_got))
        grad_hidden, *down_z = tie(grad_hidden, *down_z)
        down_zgot = [along_z(v, s) for s, v in zip((1, 2, 3), down_z[1:])]
        theirs = outer(normed_two_t, grad_hidden, 1 - mine, 4, 2)
        up_sent = over_core(theirs)
        up_mine = outer(normed_two_t, grad_hidden, mine, 4, 2)
        up_pieces = fold_core(up_mine, up_sent)
        up_mine, *down_zgot = tie(up_mine, *down_zgot)
        down_f = fold_z(down_z[0], down_zgot)
        grad_hidden, down_f, *up_pieces = tie(grad_hidden, down_f, *up_pieces)
        down_quarters = [over_dp(down_f, k) for k in (1, 2, 3)]
        up_got = [over_dp(v, k) for k, v in zip((1, 2, 3), up_pieces[1:])]
    else:
        up_full = outer(normed_two_t, grad_hidden, whole, 1, 1)[0]
    grad_resid, grad_branch, grad_mix, sums_two = second_back(
        grad_hidden, full_up, resid, given, vec, full_out
    )
    out_full = outer(mix_t, grad_branch, whole, 1, 1)[0]
    if fast:
        out_rows = scatter(out_full)
        grad_mix, down_f, *down_quarters = tie(grad_mix, down_f, *down_quarters)
        down_grad = share(down_f, down_quarters)
    projs = []
    sums_proj = []
    sums_freq = []
    qkv_parts = []
    chains = []
    for part in range(count):
        dq, dk, dv = attend_back(part, qkv, grad_mix, mix, lb, aug_q, aug_k, rng)
        if fast and part == 0:
            dq, *up_got = tie(dq, *up_got)
            up_z = fold_dp((up_pieces[0], up_got))
            dq, *up_z = tie(dq, *up_z)
            up_zgot = [along_z(v, s) for s, v in zip((1, 2, 3), up_z[1:])]
        gp, bs, fs = turn_back(part, dq, dk, dv, qkv, cos, sin, grid_t)
        projs.append(gp)
        sums_proj.append(bs)
        sums_freq.append(fs)
        if not fast:
            qkv_parts.append(outer(normed_t, gp, whole, 1, 1)[0])
            continue
        theirs = outer(normed_t, gp, 1 - mine, 4, 2)
        sent = over_core(theirs)
        own = outer(normed_t, gp, mine, 4, 2)
        pieces = fold_core(own, sent)
        if part < count - 1:
            own, *up_zgot = tie(own, *up_zgot)
            up_f = fold_z(up_z[0], up_zgot)
            grad_mix, up_f, *pieces = tie(grad_mix, up_f, *pieces)
            up_quarters = [over_dp(up_f, k) for k in (1, 2, 3)]
            got = [over_dp(v, k) for k, v in zip((1, 2, 3), pieces[1:])]
            chains.append((pieces, got))
        else:
            theirs, up_f, out_rows, *up_quarters = tie(theirs, up_f, out_rows, *up_quarters)
            projs[-1], *pieces = tie(projs[-1], *pieces)
            got = [over_dp(v, k) for k, v in zip((1, 2, 3), pieces[1:])]
            chains.append((pieces, got))
    tokens_grad, sums_one = first_back(projs, full_qkv, tokens, grad_resid, vec)
    join = lambda rows: jnp.concatenate(rows, axis=-1)
    freq_sums = join([s[:2] for s in sums_freq]).reshape(2, heads, 2, HD // 2)
    vector_full = jnp.concatenate(
        [
            sums_one[0],
            sums_one[1],
            sums_two[0],
            sums_two[1],
            join([s[:3] for s in sums_proj]).reshape(-1),
            sums_two[2],
            grad_bias_up.reshape(-1),
            grad_bias_down,
            (freq_sums[:, :, 0] - freq_sums[:, :, 1]).reshape(-1),
        ]
    )
    size = vectors.shape[0]
    if fast:
        up_grad = share(up_f, up_quarters)
        out_grad = up(sum_dp_low(out_rows))
        done = []
        for pieces, got in chains:
            zs = fold_dp((pieces[0], got))
            f = fold_z(zs[0], [along_z(v, s) for s, v in zip((1, 2, 3), zs[1:])])
            done.append(share(f, [over_dp(f, k) for k in (1, 2, 3)]))
        both = jnp.concatenate([vector_full, weight_local * 0.25]).reshape(1, -1)
        both = sum_fsdp(sum_dp(both)).reshape(-1)
        vector_total, weight_squares = both[:-4], both[-4:]
        vector_grad = lax.dynamic_slice(vector_total, (lax.axis_index("fsdp") * size,), (size,))
        off = vector_total.shape[0] - 2 * w
        down_bias_grad = vector_total[off : off + w]
        total = lambda v: sum_fsdp(v.reshape(1, -1)).reshape(-1)
    else:
        give = lambda v: lax.psum(scatter(up(v)), "dp")
        up_grad, down_grad, out_grad = give(up_full), give(down_full), give(out_full)
        done = [give(v) for v in qkv_parts]
        vector_grad = give(vector_full)
        down_bias_grad = lax.psum(grad_bias_down, ("dp", "fsdp"))
        total = lambda v: lax.psum(v, "fsdp")
        weight_squares = total(weight_local)
    L = 128 * PAIRS
    qkv_grad = join([g[:, s * L : (s + 1) * L] for s in range(3) for g in done])
    weight_norms = jnp.sqrt(weight_squares)
    reduced = (qkv_grad, out_grad, up_grad, down_grad)
    steps = [
        adam_terms(reduced[k], firsts[k], seconds[k], masters[k], 0.01) for k in range(4)
    ]
    update_norms = jnp.sqrt(total(jnp.stack([jnp.sum(s[2] * s[2]) for s in steps])))
    new_list = [
        masters[k] - 0.3 * (weight_norms[k] / (update_norms[k] + 1e-06)) * steps[k][2]
        for k in range(4)
    ]
    vector_step = adam_terms(vector_grad, vector_first, vector_second, vectors, 0.0)
    return (
        output,
        tokens_grad,
        *reduced,
        vector_grad,
        down_bias_grad,
        *[s[0] for s in steps],
        vector_step[0],
        *[s[1] for s in steps],
        vector_step[1],
        *new_list,
        vectors - 0.2 * vector_step[2],
        weight_norms,
        update_norms,
    )


def solution(mesh):
    both = P(("dp", "fsdp"), None)
    mat = [P("fsdp", None)] * 4 + [P("fsdp")]
    in_specs = (both, both, P(("dp", "fsdp")), P(None, ("dp", "fsdp")), *mat, *mat, *mat)
    out_specs = (both, both, *mat, P(), *mat, *mat, *mat, P(), P())
    fast = mesh.shape["dp"] == 4 and mesh.shape["fsdp"] == 8
    return jax.shard_map(
        partial(body, fast), mesh=mesh, in_specs=in_specs, out_specs=out_specs, check_vma=False
    )
```

time: 943 us -> 465 us (0.49)
  matrix products: 338 us -> 0 us
  Pallas kernels: 0 us -> 206 us
  waiting for transfers between devices: 277 us -> 71.4 us
  blocking collectives: 109 us -> 0 us
  starting transfers between devices: 0.37 us -> 78.5 us
  local copies, waits for them, and re-layouts: 86 us -> 30.6 us
  other arithmetic: 99.2 us -> 49.6 us
    dot_general x96 -> x0, matrix products: 338 us -> none  [the longest x40 114 us: against_columns(): lax.dot_general(left, right, (((1,), (1,)), ((), ())), preferred_element_...]
    reduce_scatter x4 -> x1, waiting for transfers between devices: 232 us -> 0.01 us  [body(): lax.psum_scatter(v, 'fsdp', scatter_dimension=0, tiled=True)]
    pallas_call x0 -> x24, Pallas kernels: none -> 206 us  [the longest x2 36.6 us: attend_back(): pl.pallas_call(attend_back_kernel, name='attend_back', grid_spec=spec, ou...]
    ppermute x0 -> x73, starting transfers between devices: none -> 78.3 us  [the longest x34 39.9 us: over_dp(): return lax.ppermute(v, 'dp', [(i, i ^ k) for i in range(4)])]
    unnamed x2 -> x0, blocking collectives: 61.9 us -> none
    ppermute x0 -> x73, waiting for transfers between devices: none -> 56.9 us  [the longest x18 25.9 us: along_z(): return lax.ppermute(v, 'fsdp', [(i, (i + 2 * s) % 8) for i in range(8)])]
    psum x2 -> x0, blocking collectives: 47.2 us -> none  [the longest x1 38.1 us: body(): down_bias_grad = lax.psum(grad_bias_down, ('dp', 'fsdp'))]
    psum x1 -> x0, waiting for transfers between devices: 40.9 us -> none  [body(): lax.psum((group_grads[0], group_grads[1], group_grads[2], group_grads[3],...]
  transfers between devices with their start and end apart: 9 -> 76, of which waited for: 5 -> 27; matrix products, arithmetic and copies ran while one was open for 45% -> 9% of each run, Pallas kernels for 0% -> 38%
where the time goes in v2:
time: 465 us; the launch traced here: 456 us
  Pallas kernels  206 us (44%)
  starting transfers between devices  78.5 us (17%)
  waiting for transfers between devices  71.4 us (15%)
  other arithmetic  49.6 us (11%)
  local copies, waits for them, and re-layouts  30.6 us (7%)
  between operations  20.4 us (4%)
    ppermute x34, starting transfers between devices, over_dp(): return lax.ppermute(v, 'dp', [(i, i ^ k) for i in range(4)])  39.9 us
    pallas_call x2, Pallas kernels, attend_back(): pl.pallas_call(attend_back_kernel, name='attend_back', grid_spec=spec, ou...  36.6 us
    pallas_call x9, Pallas kernels, outer(): pl.pallas_call(outer_kernel, name='outer', grid_spec=spec, out_shape=shap...  36.4 us
    ppermute x18, starting transfers between devices, along_z(): return lax.ppermute(v, 'fsdp', [(i, (i + 2 * s) % 8) for i in range(8)])  28.8 us
    ppermute x18, waiting for transfers between devices, along_z(): return lax.ppermute(v, 'fsdp', [(i, (i + 2 * s) % 8) for i in range(8)])  25.9 us
    ppermute x34, waiting for transfers between devices, over_dp(): return lax.ppermute(v, 'dp', [(i, i ^ k) for i in range(4)])  21.7 us
    unnamed x144, local copies, waits for them, and re-layouts  19.9 us
    pallas_call x1, Pallas kernels, hidden_units(): pl.pallas_call(hidden_kernel, name='hidden', grid=(ff // B,), in_specs=[p...  18.6 us
  transfers between devices with their start and end apart: 76, of which 27 were waited for; matrix products, arithmetic and copies ran while one was open for 9% of the time, Pallas kernels for 38%

profile of v2, /device:TPU:0, one launch (start us, length us, event | category | flops | bytes accessed | tf_op | source)
XLA Modules:
  0.0 456.0 jit_solution(11425668822158553351)
XLA Ops:
  9.9 5.1 %collective-permute-start.5 = (bf16[24,2304]{1,0:T(8,128)(2,1)S(1)}, bf16[24,2304]{1,0:T(8,128)(2,1)S(1)}, u32[]{:S(2)}, u32[]{:S(2)}) collective-permute-start(bf16[24,2304]{1,0:T(8,128)(2,1)S(1)} %dynamic-slice_convert_fusion.1), channel_id=1, source_target_pairs={{0,6},{1,7},{2,0},{3,1},{4,2},{5,3},{6,4},{7,5},{8,14},{9,15},{10,... | collective-permute-start | bytes 331784 | tf_op jit(solution)/shard_map/ppermute | solution.py:646
  22.5 14.4 %all-gather.3.cloned.1.call-done.w_ref.wo_ref = bf16[768,768]{1,0:T(8,128)(2,1)} async-done(((bf16[96,768]{1,0:T(8,128)(2,1)}), bf16[768,768]{1,0:T(8,128)(2,1)}) %all-gather.3.cloned.1.call-update) | async-done | bytes 1179664 | tf_op jit(solution)/shard_map/all_gather | solution.py:791
  39.9 2.2 collective-permute-done.1
  50.0 2.2 collective-permute-start.11
  52.5 5.6 %collective-permute-done.6.refs_1_ = bf16[4,24,2304]{2,1,0:T(8,128)(2,1)} collective-permute-done((bf16[4,24,2304]{2,1,0:T(8,128)(2,1)}, bf16[4,24,2304]{2,1,0:T(8,128)(2,1)}, u32[]{:S(2)}, u32[]{:S(2)}) %collective-permute-start.6) | collective-permute-done | bytes 442400 | tf_op jit(solution)/shard_map/ppermute | solution.py:634
  59.1 14.5 %first.1 = (bf16[1024,768]{1,0:T(8,128)(2,1)S(1)}, bf16[768,1024]{1,0:T(8,128)(2,1)S(1)}, f32[1024,768]{1,0:T(8,128)}, f32[1024,768]{1,0:T(8,128)}) custom-call(bf16[1024,768]{1,0:T(8,128)(2,1)S(1)} %copy-done.9, f32[1,10752]{1,0:T(1,128)S(1)} %reshape.364.vec_ref.b_ref.refs_5_, f32[2,768]{1,0:T(2,128)S(1)} %reshape.348.freq_ref, f32[1024,2]{1,0:T(8,128)S(1)} %bitcast.138), custom_call_target="tpu_custom_call" | custom-call | flops 10000000000 | bytes 10000000 | tf_op jit(solution)/shard_map/first/pallas_call | solution.py:76
  74.3 7.6 %collective-permute-done.10 = bf16[24,3072]{1,0:T(8,128)(2,1)S(1)} collective-permute-done((bf16[24,3072]{1,0:T(8,128)(2,1)S(1)}, bf16[24,3072]{1,0:T(8,128)(2,1)S(1)}, u32[]{:S(2)}, u32[]{:S(2)}) %collective-permute-start.10) | collective-permute-done | bytes 147488 | tf_op jit(solution)/shard_map/ppermute | solution.py:646
  83.7 4.2 arrange.2
  91.3 13.4 %project.1.q_ref.k_ref.v_ref = bf16[1024,2304]{1,0:T(8,128)(2,1)} custom-call(bf16[1024,768]{1,0:T(8,128)(2,1)S(1)} %get-tuple-element.133.n_ref, bf16[768,2304]{1,0:T(8,128)(2,1)} %bitcast.153, f32[1,10752]{1,0:T(1,128)S(1)} %reshape.364.vec_ref.b_ref.refs_5_, f32[1024,768]{1,0:T(8,128)S(1)} %copy-done, f32[1024,768]{1,0:T(8,128)} %get-tuple-element.141.sin_ref), custom_call_target="tpu_custom_call" | custom-call | flops 8000000000 | bytes 10000000 | tf_op jit(solution)/shard_map/project/pallas_call | solution.py:110
  104.7 16.8 %attend.1 = (bf16[1024,768]{1,0:T(8,128)(2,1)S(1)}, bf16[768,1024]{1,0:T(8,128)(2,1)S(1)}, f32[6,8,1024]{2,1,0:T(8,128)S(1)}) custom-call(s32[2,4]{1,0:T(2,128)S(1)} %pad_add_fusion.rng, bf16[1024,2304]{1,0:T(8,128)(2,1)} %project.1.q_ref.k_ref.v_ref, bf16[1024,2304]{1,0:T(8,128)(2,1)} %project.1.q_ref.k_ref.v_ref, ...), custom_call_target="tpu_custom_call" | custom-call | flops 23000000512 | bytes 10000000 | tf_op jit(solution)/shard_map/attend/pallas_call | solution.py:220
  126.0 5.5 %branch.1 = (f32[1024,768]{1,0:T(8,128)}, bf16[1024,768]{1,0:T(8,128)(2,1)S(1)}, bf16[768,1024]{1,0:T(8,128)(2,1)S(1)}) custom-call(bf16[1024,768]{1,0:T(8,128)(2,1)S(1)} %copy-done.10, bf16[1024,768]{1,0:T(8,128)(2,1)} %copy-done.23, bf16[768,768]{1,0:T(8,128)(2,1)S(1)} %copy-done.12, f32[1,10752]{1,0:T(1,128)S(1)} %reshape.364.vec_ref.b_ref.refs_5_), custom_call_target="tpu_custom_call" | custom-call | flops 4000000000 | bytes 10000000 | tf_op jit(solution)/shard_map/branch/pallas_call | solution.py:354
  133.9 3.5 arrange.3
  137.5 18.6 %hidden.1 = (bf16[1024,3072]{1,0:T(8,128)(2,1)}, bf16[3072,1024]{1,0:T(8,128)(2,1)}, bf16[1024,3072]{1,0:T(8,128)(2,1)}) custom-call(bf16[1024,768]{1,0:T(8,128)(2,1)S(1)} %copy-done.25, bf16[768,3072]{1,0:T(8,128)(2,1)} %bitcast.151, f32[1,10752]{1,0:T(1,128)S(1)} %reshape.364.vec_ref.b_ref.refs_5_), custom_call_target="tpu_custom_call" | custom-call | flops 15000000512 | bytes 10000000 | tf_op jit(solution)/shard_map/hidden/pallas_call | solution.py:397
  156.1 6.3 %outer.10 = bf16[4,384,768]{2,1,0:T(8,128)(2,1)} custom-call(s32[1]{0:T(128)S(6)} %sub.83.sel, bf16[4,2,384,1024]{3,2,1,0:T(8,128)(2,1)} %bitcast.165, bf16[1024,768]{1,0:T(8,128)(2,1)S(1)} %get-tuple-element.269.y_ref.g_ref.cot_ref), custom_call_target="tpu_custom_call" | custom-call | flops 4831838208 | bytes 10000000 | tf_op jit(solution)/shard_map/outer/pallas_call | solution.py:538
  162.5 5.1 %outer.9 = bf16[4,384,768]{2,1,0:T(8,128)(2,1)S(1)} custom-call(s32[1]{0:T(128)} %bitcast.13.sel, bf16[4,2,384,1024]{3,2,1,0:T(8,128)(2,1)} %bitcast.166, bf16[1024,768]{1,0:T(8,128)(2,1)S(1)} %get-tuple-element.269.y_ref.g_ref.cot_ref), custom_call_target="tpu_custom_call" | custom-call | flops 4831838208 | bytes 10000000 | tf_op jit(solution)/shard_map/outer/pallas_call | solution.py:538
  167.6 2.3 add_convert_fusion.1
  170.3 2.7 collective-permute-start.25
  174.4 10.8 %hidden_back.1 = (bf16[1024,3072]{1,0:T(8,128)(2,1)}, f32[1,3072]{1,0:T(1,128)S(1)}) custom-call(bf16[1024,768]{1,0:T(8,128)(2,1)S(1)} %get-tuple-element.269.y_ref.g_ref.cot_ref, bf16[3072,768]{1,0:T(8,128)(2,1)} %all-gather.5.cloned.1.call-done.w_ref, bf16[1024,3072]{1,0:T(8,128)(2,1)} %get-tuple-element.158.d_ref), custom_call_target="tpu_custom_call" | custom-call | flops 8000000000 | bytes 10000000 | tf_op jit(solution)/shard_map/hidden_back/pallas_call | solution.py:452
  185.2 9.4 %last.1 = bf16[1024,768]{1,0:T(8,128)(2,1)} custom-call(bf16[1024,3072]{1,0:T(8,128)(2,1)} %get-tuple-element.155.a_ref, bf16[3072,768]{1,0:T(8,128)(2,1)} %all-gather.5.cloned.1.call-done.w_ref, f32[1024,768]{1,0:T(8,128)S(1)} %copy-done.22, f32[1,10752]{1,0:T(1,128)S(1)} %reshape.364.vec_ref.b_ref.refs_5_), custom_call_target="tpu_custom_call" | custom-call | flops 6000000000 | bytes 10000000 | tf_op jit(solution)/shard_map/last/pallas_call | solution.py:425
  194.6 4.2 collective-permute-done.25
  202.1 7.2 %outer.12 = bf16[4,96,3072]{2,1,0:T(8,128)(2,1)} custom-call(s32[1]{0:T(128)S(6)} %sub.83.sel, bf16[4,2,96,1024]{3,2,1,0:T(8,128)(2,1)S(1)} %bitcast.147, bf16[1024,3072]{1,0:T(8,128)(2,1)} %get-tuple-element.178.y_ref.gh_ref), custom_call_target="tpu_custom_call" | custom-call | flops 4831838208 | bytes 10000000 | tf_op jit(solution)/shard_map/outer/pallas_call | solution.py:538
  209.4 3.7 collective-permute-start.29
  214.5 6.2 %outer.11 = bf16[4,96,3072]{2,1,0:T(8,128)(2,1)S(1)} custom-call(s32[1]{0:T(128)} %bitcast.13.sel, bf16[4,2,96,1024]{3,2,1,0:T(8,128)(2,1)S(1)} %bitcast.148, bf16[1024,3072]{1,0:T(8,128)(2,1)} %get-tuple-element.178.y_ref.gh_ref), custom_call_target="tpu_custom_call" | custom-call | flops 4831838208 | bytes 10000000 | tf_op jit(solution)/shard_map/outer/pallas_call | solution.py:538
  220.8 2.5 collective-permute-done.28
  223.4 2.6 add_convert_fusion
  233.0 14.6 %second_back.1 = (f32[1024,768]{1,0:T(8,128)}, bf16[1024,768]{1,0:T(8,128)(2,1)S(1)}, bf16[1024,768]{1,0:T(8,128)(2,1)S(1)}, f32[8,768]{1,0:T(8,128)S(1)}) custom-call(bf16[1024,3072]{1,0:T(8,128)(2,1)} %get-tuple-element.178.y_ref.gh_ref, bf16[768,3072]{1,0:T(8,128)(2,1)} %bitcast.152, f32[1024,768]{1,0:T(8,128)} %get-tuple-element.157.res_ref, ...), custom_call_target="tpu_custom_call" | custom-call | flops 8999999488 | bytes 10000000 | tf_op jit(solution)/shard_map/second_back/pallas_call | solution.py:506
  248.7 3.0 outer.17
  253.5 18.1 %attend_back.2 = (f32[1024,384]{1,0:T(8,128)S(1)}, f32[1024,384]{1,0:T(8,128)S(1)}, bf16[1024,384]{1,0:T(8,128)(2,1)S(1)}) custom-call(s32[2,4]{1,0:T(2,128)S(1)} %pad_add_fusion.rng, bf16[1024,2304]{1,0:T(8,128)(2,1)} %project.1.q_ref.k_ref.v_ref, bf16[1024,2304]{1,0:T(8,128)(2,1)} %project.1.q_ref.k_ref.v_ref, ...), custom_call_target="tpu_custom_call" | custom-call | flops 22000001024 | bytes 10000000 | tf_op jit(solution)/shard_map/attend_back/pallas_call | solution.py:330
  275.3 6.1 %turn_back.2 = (bf16[1024,1152]{1,0:T(8,128)(2,1)}, f32[8,384]{1,0:T(8,128)S(1)}, f32[8,384]{1,0:T(8,128)S(1)}) custom-call(f32[1024,384]{1,0:T(8,128)S(1)} %get-tuple-element.192.dq_ref, f32[1024,384]{1,0:T(8,128)S(1)} %get-tuple-element.193.dk_ref, bf16[1024,384]{1,0:T(8,128)(2,1)S(1)} %get-tuple-element.194.dv_ref, ...), custom_call_target="tpu_custom_call" | custom-call | flops 4000000000 | bytes 10000000 | tf_op jit(solution)/shard_map/turn_back/pallas_call | solution.py:583
  285.4 3.0 multiply_reduce_fusion
  288.4 2.4 collective-permute-start.37
  297.1 6.1 %collective-permute-done.38 = bf16[24,3072]{1,0:T(8,128)(2,1)S(1)} collective-permute-done((bf16[24,3072]{1,0:T(8,128)(2,1)S(1)}, bf16[24,3072]{1,0:T(8,128)(2,1)S(1)}, u32[]{:S(2)}, u32[]{:S(2)}) %collective-permute-start.38) | collective-permute-done | bytes 147488 | tf_op jit(solution)/shard_map/ppermute | solution.py:646
  306.6 18.5 %attend_back.3 = (f32[1024,384]{1,0:T(8,128)S(1)}, f32[1024,384]{1,0:T(8,128)S(1)}, bf16[1024,384]{1,0:T(8,128)(2,1)S(1)}) custom-call(s32[2,4]{1,0:T(2,128)S(1)} %pad_add_fusion.rng, bf16[1024,2304]{1,0:T(8,128)(2,1)} %project.1.q_ref.k_ref.v_ref, bf16[1024,2304]{1,0:T(8,128)(2,1)} %project.1.q_ref.k_ref.v_ref, ...), custom_call_target="tpu_custom_call" | custom-call | flops 22000001024 | bytes 10000000 | tf_op jit(solution)/shard_map/attend_back/pallas_call | solution.py:330
  325.1 6.1 %turn_back.3 = (bf16[1024,1152]{1,0:T(8,128)(2,1)}, f32[8,384]{1,0:T(8,128)S(1)}, f32[8,384]{1,0:T(8,128)S(1)}) custom-call(f32[1024,384]{1,0:T(8,128)S(1)} %get-tuple-element.205.dq_ref, f32[1024,384]{1,0:T(8,128)S(1)} %get-tuple-element.206.dk_ref, bf16[1024,384]{1,0:T(8,128)(2,1)S(1)} %get-tuple-element.207.dv_ref, ...), custom_call_target="tpu_custom_call" | custom-call | flops 4000000000 | bytes 10000000 | tf_op jit(solution)/shard_map/turn_back/pallas_call | solution.py:583
  344.7 3.3 collective-permute-done.43
  349.3 5.5 %collective-permute-start.47 = (bf16[24,1152]{1,0:T(8,128)(2,1)S(1)}, bf16[24,1152]{1,0:T(8,128)(2,1)S(1)}, u32[]{:S(2)}, u32[]{:S(2)}) collective-permute-start(bf16[24,1152]{1,0:T(8,128)(2,1)S(1)} %get-tuple-element.314), channel_id=1, source_target_pairs={{0,6},{1,7},{2,0},{3,1},{4,2},{5,3},{6,4},{7,5},{8,14},{9,15},{10,... | collective-permute-start | bytes 165896 | tf_op jit(solution)/shard_map/ppermute | solution.py:646
  356.6 3.2 collective-permute-done.46
  370.9 2.6 collective-permute-start.53
  377.5 9.0 %first_back.1 = (bf16[1024,768]{1,0:T(8,128)(2,1)}, f32[8,768]{1,0:T(8,128)S(1)}) custom-call(bf16[1024,1152]{1,0:T(8,128)(2,1)S(1)} %copy-done.6, bf16[1024,1152]{1,0:T(8,128)(2,1)} %get-tuple-element.209.y_ref.refs_1_, bf16[768,2304]{1,0:T(8,128)(2,1)} %bitcast.154, bf16[1024,768]{1,0:T(8,128)(2,1)S(1)} %copy-done.11, ...), custom_call_target="tpu_custom_call" | custom-call | flops 7000000000 | bytes 10000000 | tf_op jit(solution)/shard_map/first_back/pallas_call | solution.py:621
  388.1 2.6 multiply_reduce_fusion.1
  390.8 2.2 add_convert_fusion.6
  411.5 2.7 constant_dynamic-update-slice_fusion.3
  415.2 2.7 maximum_bitcast_fusion
  419.1 2.7 fusion.27
  422.6 2.7 collective-permute-done.71
  425.3 2.7 fusion.29
  430.2 2.2 collective-permute-done.72
  432.9 2.2 collective-permute-start.69
  (378 shorter events, 134.8 us)
Async XLA Ops:
  7.2 29.7 %all-gather.3.cloned.1.call-start = ((), (), s32[]{:S(2)}) async-start(), calls=%async_computation.1 | async-start | bytes 1327104 | tf_op jit(solution)/shard_map/all_gather | solution.py:791
  8.9 128.6 %all-gather.5.cloned.1.call-start = ((), (), s32[]{:S(2)}) async-start(), calls=%async_computation.2 | async-start | bytes 5308416 | tf_op jit(solution)/shard_map/all_gather | solution.py:791
  9.9 34.0 %collective-permute-start.5 = (bf16[24,2304]{1,0:T(8,128)(2,1)S(1)}, bf16[24,2304]{1,0:T(8,128)(2,1)S(1)}, u32[]{:S(2)}, u32[]{:S(2)}) collective-permute-start(bf16[24,2304]{1,0:T(8,128)(2,1)S(1)} %dynamic-slice_convert_fusion.1), channel_id=1, source_target_pairs={{0,6},{1,7},{2,0},{3,1},{4,2},{5,3},{6,4},{7,5},{8,14},{9,15},{10,... | collective-permute-start | bytes 331784 | tf_op jit(solution)/shard_map/ppermute | solution.py:646
  15.0 28.9 %collective-permute-start.4 = (bf16[24,2304]{1,0:T(8,128)(2,1)S(1)}, bf16[24,2304]{1,0:T(8,128)(2,1)S(1)}, u32[]{:S(2)}, u32[]{:S(2)}) collective-permute-start(bf16[24,2304]{1,0:T(8,128)(2,1)S(1)} %dynamic-slice_convert_fusion.1), channel_id=1, source_target_pairs={{0,4},{1,5},{2,6},{3,7},{4,0},{5,1},{6,2},{7,3},{8,12},{9,13},{10,... | collective-permute-start | bytes 331784 | tf_op jit(solution)/shard_map/ppermute | solution.py:646
  15.0 28.9 %collective-permute-start.3 = (bf16[24,2304]{1,0:T(8,128)(2,1)S(1)}, bf16[24,2304]{1,0:T(8,128)(2,1)S(1)}, u32[]{:S(2)}, u32[]{:S(2)}) collective-permute-start(bf16[24,2304]{1,0:T(8,128)(2,1)S(1)} %dynamic-slice_convert_fusion.1), channel_id=1, source_target_pairs={{0,2},{1,3},{2,4},{3,5},{4,6},{5,7},{6,0},{7,1},{8,10},{9,11},{10,... | collective-permute-start | bytes 331784 | tf_op jit(solution)/shard_map/ppermute | solution.py:646
  16.8 21.5 %collective-permute-start = (bf16[1,1344]{1,0:T(2,128)(2,1)S(1)}, bf16[1,1344]{1,0:T(2,128)(2,1)S(1)}, u32[]{:S(2)}, u32[]{:S(2)}) collective-permute-start(bf16[1,1344]{1,0:T(2,128)(2,1)S(1)} %reshape.347), channel_id=1, source_target_pairs={{0,1},{1,0},{2,3},{3,2},{4,5},{5,4},{6,7},{7,6},{8,9},{9,8},{10,11... | collective-permute-start | bytes 8072 | tf_op jit(solution)/shard_map/ppermute | solution.py:638
  36.9 337.5 %reduce-scatter.2.cloned.1.call-start = ((), (), s32[]{:S(2)}) async-start(), calls=%async_computation.3 | async-start | bytes 1327104 | tf_op jit(solution)/shard_map/reduce_scatter | solution.py:792
  44.7 13.4 %collective-permute-start.6 = (bf16[4,24,2304]{2,1,0:T(8,128)(2,1)}, bf16[4,24,2304]{2,1,0:T(8,128)(2,1)}, u32[]{:S(2)}, u32[]{:S(2)}) collective-permute-start(bf16[4,24,2304]{2,1,0:T(8,128)(2,1)} %pad_maximum_fusion.1.refs_0_), channel_id=1, source_target_pairs={{0,8},{8,0},{16,24},{24,16},{1,9},{9,1},{17,25},{25,17},{2,10},{10... | collective-permute-start | bytes 1327112 | tf_op jit(solution)/shard_map/ppermute | solution.py:634
  47.1 26.5 %collective-permute-start.7 = (bf16[4,24,2304]{2,1,0:T(8,128)(2,1)}, bf16[4,24,2304]{2,1,0:T(8,128)(2,1)S(1)}, u32[]{:S(2)}, u32[]{:S(2)}) collective-permute-start(bf16[4,24,2304]{2,1,0:T(8,128)(2,1)} %pad_maximum_fusion.1.refs_0_), channel_id=1, source_target_pairs={{0,16},{8,24},{16,0},{24,8},{1,17},{9,25},{17,1},{25,9},{2,18},{10... | collective-permute-start | bytes 1327112 | tf_op jit(solution)/shard_map/ppermute | solution.py:634
  48.5 25.1 %collective-permute-start.8 = (bf16[4,24,2304]{2,1,0:T(8,128)(2,1)}, bf16[4,24,2304]{2,1,0:T(8,128)(2,1)S(1)}, u32[]{:S(2)}, u32[]{:S(2)}) collective-permute-start(bf16[4,24,2304]{2,1,0:T(8,128)(2,1)} %pad_maximum_fusion.1.refs_0_), channel_id=1, source_target_pairs={{0,24},{8,16},{16,8},{24,0},{1,25},{9,17},{17,9},{25,1},{2,26},{10... | collective-permute-start | bytes 1327112 | tf_op jit(solution)/shard_map/ppermute | solution.py:634
  50.0 24.2 %collective-permute-start.11 = (bf16[24,3072]{1,0:T(8,128)(2,1)S(1)}, bf16[24,3072]{1,0:T(8,128)(2,1)S(1)}, u32[]{:S(2)}, u32[]{:S(2)}) collective-permute-start(bf16[24,3072]{1,0:T(8,128)(2,1)S(1)} %dynamic-slice_convert_fusion), channel_id=1, source_target_pairs={{0,6},{1,7},{2,0},{3,1},{4,2},{5,3},{6,4},{7,5},{8,14},{9,15},{10,... | collective-permute-start | bytes 442376 | tf_op jit(solution)/shard_map/ppermute | solution.py:646
  52.2 29.7 %collective-permute-start.10 = (bf16[24,3072]{1,0:T(8,128)(2,1)S(1)}, bf16[24,3072]{1,0:T(8,128)(2,1)S(1)}, u32[]{:S(2)}, u32[]{:S(2)}) collective-permute-start(bf16[24,3072]{1,0:T(8,128)(2,1)S(1)} %dynamic-slice_convert_fusion), channel_id=1, source_target_pairs={{0,4},{1,5},{2,6},{3,7},{4,0},{5,1},{6,2},{7,3},{8,12},{9,13},{10,... | collective-permute-start | bytes 442376 | tf_op jit(solution)/shard_map/ppermute | solution.py:646
  58.2 23.8 %collective-permute-start.9 = (bf16[24,3072]{1,0:T(8,128)(2,1)S(1)}, bf16[24,3072]{1,0:T(8,128)(2,1)S(1)}, u32[]{:S(2)}, u32[]{:S(2)}) collective-permute-start(bf16[24,3072]{1,0:T(8,128)(2,1)S(1)} %dynamic-slice_convert_fusion), channel_id=1, source_target_pairs={{0,2},{1,3},{2,4},{3,5},{4,6},{5,7},{6,0},{7,1},{8,10},{9,11},{10,... | collective-permute-start | bytes 442376 | tf_op jit(solution)/shard_map/ppermute | solution.py:646
  73.6 8.4 %collective-permute-start.12 = (bf16[4,24,2304]{2,1,0:T(8,128)(2,1)}, bf16[4,24,2304]{2,1,0:T(8,128)(2,1)S(1)}, u32[]{:S(2)}, u32[]{:S(2)}) collective-permute-start(bf16[4,24,2304]{2,1,0:T(8,128)(2,1)} %pad_maximum_fusion.1.refs_0_), channel_id=1, source_target_pairs={{0,1},{1,0},{2,3},{3,2},{4,5},{5,4},{6,7},{7,6},{8,9},{9,8},{10,11... | collective-permute-start | bytes 1327112 | tf_op jit(solution)/shard_map/ppermute | solution.py:638
  87.9 36.0 %collective-permute-start.16 = (bf16[4,24,3072]{2,1,0:T(8,128)(2,1)S(1)}, bf16[4,24,3072]{2,1,0:T(8,128)(2,1)S(1)}, u32[]{:S(2)}, u32[]{:S(2)}) collective-permute-start(bf16[4,24,3072]{2,1,0:T(8,128)(2,1)S(1)} %pad_maximum_fusion.refs_0_), channel_id=1, source_target_pairs={{0,8},{8,0},{16,24},{24,16},{1,9},{9,1},{17,25},{25,17},{2,10},{10... | collective-permute-start | bytes 1769480 | tf_op jit(solution)/shard_map/ppermute | solution.py:634
  87.9 36.0 %collective-permute-start.17 = (bf16[4,24,3072]{2,1,0:T(8,128)(2,1)S(1)}, bf16[4,24,3072]{2,1,0:T(8,128)(2,1)S(1)}, u32[]{:S(2)}, u32[]{:S(2)}) collective-permute-start(bf16[4,24,3072]{2,1,0:T(8,128)(2,1)S(1)} %pad_maximum_fusion.refs_0_), channel_id=1, source_target_pairs={{0,16},{8,24},{16,0},{24,8},{1,17},{9,25},{17,1},{25,9},{2,18},{10... | collective-permute-start | bytes 1769480 | tf_op jit(solution)/shard_map/ppermute | solution.py:634
  89.5 34.4 %collective-permute-start.18 = (bf16[4,24,3072]{2,1,0:T(8,128)(2,1)S(1)}, bf16[4,24,3072]{2,1,0:T(8,128)(2,1)S(1)}, u32[]{:S(2)}, u32[]{:S(2)}) collective-permute-start(bf16[4,24,3072]{2,1,0:T(8,128)(2,1)S(1)} %pad_maximum_fusion.refs_0_), channel_id=1, source_target_pairs={{0,24},{8,16},{16,8},{24,0},{1,25},{9,17},{17,9},{25,1},{2,26},{10... | collective-permute-start | bytes 1769480 | tf_op jit(solution)/shard_map/ppermute | solution.py:634
  123.9 10.0 %collective-permute-start.19 = (bf16[4,24,3072]{2,1,0:T(8,128)(2,1)S(1)}, bf16[4,24,3072]{2,1,0:T(8,128)(2,1)S(1)}, u32[]{:S(2)}, u32[]{:S(2)}) collective-permute-start(bf16[4,24,3072]{2,1,0:T(8,128)(2,1)S(1)} %pad_maximum_fusion.refs_0_), channel_id=1, source_target_pairs={{0,1},{1,0},{2,3},{3,2},{4,5},{5,4},{6,7},{7,6},{8,9},{9,8},{10,11... | collective-permute-start | bytes 1769480 | tf_op jit(solution)/shard_map/ppermute | solution.py:638
  124.0 9.9 %collective-permute-start.20 = (bf16[4,24,3072]{2,1,0:T(8,128)(2,1)S(1)}, bf16[4,24,3072]{2,1,0:T(8,128)(2,1)S(1)}, u32[]{:S(2)}, u32[]{:S(2)}) collective-permute-start(bf16[4,24,3072]{2,1,0:T(8,128)(2,1)S(1)} %collective-permute-done.16.refs_1_), channel_id=1, source_target_pairs={{0,1},{1,0},{2,3},{3,2},{4,5},{5,4},{6,7},{7,6},{8,9},{9,8},{10,11... | collective-permute-start | bytes 1769480 | tf_op jit(solution)/shard_map/ppermute | solution.py:638
  124.5 9.4 %collective-permute-start.21 = (bf16[4,24,3072]{2,1,0:T(8,128)(2,1)S(1)}, bf16[4,24,3072]{2,1,0:T(8,128)(2,1)S(1)}, u32[]{:S(2)}, u32[]{:S(2)}) collective-permute-start(bf16[4,24,3072]{2,1,0:T(8,128)(2,1)S(1)} %collective-permute-done.17.refs_2_), channel_id=1, source_target_pairs={{0,1},{1,0},{2,3},{3,2},{4,5},{5,4},{6,7},{7,6},{8,9},{9,8},{10,11... | collective-permute-start | bytes 1769480 | tf_op jit(solution)/shard_map/ppermute | solution.py:638
  124.6 9.4 %collective-permute-start.22 = (bf16[4,24,3072]{2,1,0:T(8,128)(2,1)S(1)}, bf16[4,24,3072]{2,1,0:T(8,128)(2,1)S(1)}, u32[]{:S(2)}, u32[]{:S(2)}) collective-permute-start(bf16[4,24,3072]{2,1,0:T(8,128)(2,1)S(1)} %collective-permute-done.18.refs_3_), channel_id=1, source_target_pairs={{0,1},{1,0},{2,3},{3,2},{4,5},{5,4},{6,7},{7,6},{8,9},{9,8},{10,11... | collective-permute-start | bytes 1769480 | tf_op jit(solution)/shard_map/ppermute | solution.py:638
  170.1 24.5 %collective-permute-start.24 = (bf16[4,96,768]{2,1,0:T(8,128)(2,1)S(1)}, bf16[4,96,768]{2,1,0:T(8,128)(2,1)S(1)}, u32[]{:S(2)}, u32[]{:S(2)}) collective-permute-start(bf16[4,96,768]{2,1,0:T(8,128)(2,1)S(1)} %get-tuple-element.160), channel_id=1, source_target_pairs={{0,8},{8,0},{16,24},{24,16},{1,9},{9,1},{17,25},{25,17},{2,10},{10... | collective-permute-start | bytes 1769480 | tf_op jit(solution)/shard_map/ppermute | solution.py:634
  170.3 28.5 %collective-permute-start.25 = (bf16[4,96,768]{2,1,0:T(8,128)(2,1)S(1)}, bf16[4,96,768]{2,1,0:T(8,128)(2,1)S(1)}, u32[]{:S(2)}, u32[]{:S(2)}) collective-permute-start(bf16[4,96,768]{2,1,0:T(8,128)(2,1)S(1)} %get-tuple-element.161), channel_id=1, source_target_pairs={{0,16},{8,24},{16,0},{24,8},{1,17},{9,25},{17,1},{25,9},{2,18},{10... | collective-permute-start | bytes 1769480 | tf_op jit(solution)/shard_map/ppermute | solution.py:634
  173.0 27.7 %collective-permute-start.26 = (bf16[4,96,768]{2,1,0:T(8,128)(2,1)S(1)}, bf16[4,96,768]{2,1,0:T(8,128)(2,1)S(1)}, u32[]{:S(2)}, u32[]{:S(2)}) collective-permute-start(bf16[4,96,768]{2,1,0:T(8,128)(2,1)S(1)} %get-tuple-element.162), channel_id=1, source_target_pairs={{0,24},{8,16},{16,8},{24,0},{1,25},{9,17},{17,9},{25,1},{2,26},{10... | collective-permute-start | bytes 1769480 | tf_op jit(solution)/shard_map/ppermute | solution.py:634
  209.3 14.1 %collective-permute-start.30 = (bf16[4,96,3072]{2,1,0:T(8,128)(2,1)}, bf16[4,96,3072]{2,1,0:T(8,128)(2,1)}, u32[]{:S(2)}, u32[]{:S(2)}) collective-permute-start(bf16[4,96,3072]{2,1,0:T(8,128)(2,1)} %outer.12), channel_id=1, source_target_pairs={{0,1},{1,0},{2,3},{3,2},{4,5},{5,4},{6,7},{7,6},{8,9},{9,8},{10,11... | collective-permute-start | bytes 7077896 | tf_op jit(solution)/shard_map/ppermute | solution.py:638
  209.3 11.5 %collective-permute-start.27 = (bf16[96,768]{1,0:T(8,128)(2,1)S(1)}, bf16[96,768]{1,0:T(8,128)(2,1)S(1)}, u32[]{:S(2)}, u32[]{:S(2)}) collective-permute-start(bf16[96,768]{1,0:T(8,128)(2,1)S(1)} %get-tuple-element.172), channel_id=1, source_target_pairs={{0,2},{1,3},{2,4},{3,5},{4,6},{5,7},{6,0},{7,1},{8,10},{9,11},{10,... | collective-permute-start | bytes 442376 | tf_op jit(solution)/shard_map/ppermute | solution.py:646
  209.3 14.0 %collective-permute-start.28 = (bf16[96,768]{1,0:T(8,128)(2,1)S(1)}, bf16[96,768]{1,0:T(8,128)(2,1)S(1)}, u32[]{:S(2)}, u32[]{:S(2)}) collective-permute-start(bf16[96,768]{1,0:T(8,128)(2,1)S(1)} %get-tuple-element.173), channel_id=1, source_target_pairs={{0,4},{1,5},{2,6},{3,7},{4,0},{5,1},{6,2},{7,3},{8,12},{9,13},{10,... | collective-permute-start | bytes 442376 | tf_op jit(solution)/shard_map/ppermute | solution.py:646
  209.4 13.9 %collective-permute-start.29 = (bf16[96,768]{1,0:T(8,128)(2,1)S(1)}, bf16[96,768]{1,0:T(8,128)(2,1)S(1)}, u32[]{:S(2)}, u32[]{:S(2)}) collective-permute-start(bf16[96,768]{1,0:T(8,128)(2,1)S(1)} %get-tuple-element.174), channel_id=1, source_target_pairs={{0,6},{1,7},{2,0},{3,1},{4,2},{5,3},{6,4},{7,5},{8,14},{9,15},{10,... | collective-permute-start | bytes 442376 | tf_op jit(solution)/shard_map/ppermute | solution.py:646
  227.1 25.2 %collective-permute-start.31 = (bf16[96,768]{1,0:T(8,128)(2,1)S(1)}, bf16[96,768]{1,0:T(8,128)(2,1)S(1)}, u32[]{:S(2)}, u32[]{:S(2)}) collective-permute-start(bf16[96,768]{1,0:T(8,128)(2,1)S(1)} %add_convert_fusion.11), channel_id=1, source_target_pairs={{0,8},{8,0},{16,24},{24,16},{1,9},{9,1},{17,25},{25,17},{2,10},{10... | collective-permute-start | bytes 442376 | tf_op jit(solution)/shard_map/ppermute | solution.py:634
  227.7 25.8 %collective-permute-start.32 = (bf16[96,768]{1,0:T(8,128)(2,1)S(1)}, bf16[96,768]{1,0:T(8,128)(2,1)}, u32[]{:S(2)}, u32[]{:S(2)}) collective-permute-start(bf16[96,768]{1,0:T(8,128)(2,1)S(1)} %add_convert_fusion.11), channel_id=1, source_target_pairs={{0,16},{8,24},{16,0},{24,8},{1,17},{9,25},{17,1},{25,9},{2,18},{10... | collective-permute-start | bytes 442376 | tf_op jit(solution)/shard_map/ppermute | solution.py:634
  229.5 24.0 %collective-permute-start.33 = (bf16[96,768]{1,0:T(8,128)(2,1)S(1)}, bf16[96,768]{1,0:T(8,128)(2,1)}, u32[]{:S(2)}, u32[]{:S(2)}) collective-permute-start(bf16[96,768]{1,0:T(8,128)(2,1)S(1)} %add_convert_fusion.11), channel_id=1, source_target_pairs={{0,24},{8,16},{16,8},{24,0},{1,25},{9,17},{17,9},{25,1},{2,26},{10... | collective-permute-start | bytes 442376 | tf_op jit(solution)/shard_map/ppermute | solution.py:634
  230.6 42.0 %collective-permute-start.34 = (bf16[4,24,3072]{2,1,0:T(8,128)(2,1)}, bf16[4,24,3072]{2,1,0:T(8,128)(2,1)}, u32[]{:S(2)}, u32[]{:S(2)}) collective-permute-start(bf16[4,24,3072]{2,1,0:T(8,128)(2,1)} %get-tuple-element.184), channel_id=1, source_target_pairs={{0,8},{8,0},{16,24},{24,16},{1,9},{9,1},{17,25},{25,17},{2,10},{10... | collective-permute-start | bytes 1769480 | tf_op jit(solution)/shard_map/ppermute | solution.py:634
  231.2 41.5 %collective-permute-start.35 = (bf16[4,24,3072]{2,1,0:T(8,128)(2,1)}, bf16[4,24,3072]{2,1,0:T(8,128)(2,1)}, u32[]{:S(2)}, u32[]{:S(2)}) collective-permute-start(bf16[4,24,3072]{2,1,0:T(8,128)(2,1)} %get-tuple-element.185), channel_id=1, source_target_pairs={{0,16},{8,24},{16,0},{24,8},{1,17},{9,25},{17,1},{25,9},{2,18},{10... | collective-permute-start | bytes 1769480 | tf_op jit(solution)/shard_map/ppermute | solution.py:634
  252.3 20.4 %collective-permute-start.36 = (bf16[4,24,3072]{2,1,0:T(8,128)(2,1)S(1)}, bf16[4,24,3072]{2,1,0:T(8,128)(2,1)S(1)}, u32[]{:S(2)}, u32[]{:S(2)}) collective-permute-start(bf16[4,24,3072]{2,1,0:T(8,128)(2,1)S(1)} %get-tuple-element.186), channel_id=1, source_target_pairs={{0,24},{8,16},{16,8},{24,0},{1,25},{9,17},{17,9},{25,1},{2,26},{10... | collective-permute-start | bytes 1769480 | tf_op jit(solution)/shard_map/ppermute | solution.py:634
  285.3 18.6 %collective-permute-start.40 = (bf16[4,96,1152]{2,1,0:T(8,128)(2,1)S(1)}, bf16[4,96,1152]{2,1,0:T(8,128)(2,1)S(1)}, u32[]{:S(2)}, u32[]{:S(2)}) collective-permute-start(bf16[4,96,1152]{2,1,0:T(8,128)(2,1)S(1)} %outer.14), channel_id=1, source_target_pairs={{0,1},{1,0},{2,3},{3,2},{4,5},{5,4},{6,7},{7,6},{8,9},{9,8},{10,11... | collective-permute-start | bytes 2654216 | tf_op jit(solution)/shard_map/ppermute | solution.py:638
  288.4 8.7 %collective-permute-start.37 = (bf16[24,3072]{1,0:T(8,128)(2,1)S(1)}, bf16[24,3072]{1,0:T(8,128)(2,1)S(1)}, u32[]{:S(2)}, u32[]{:S(2)}) collective-permute-start(bf16[24,3072]{1,0:T(8,128)(2,1)S(1)} %get-tuple-element.198), channel_id=1, source_target_pairs={{0,2},{1,3},{2,4},{3,5},{4,6},{5,7},{6,0},{7,1},{8,10},{9,11},{10,... | collective-permute-start | bytes 442376 | tf_op jit(solution)/shard_map/ppermute | solution.py:646
  290.8 12.3 %collective-permute-start.38 = (bf16[24,3072]{1,0:T(8,128)(2,1)S(1)}, bf16[24,3072]{1,0:T(8,128)(2,1)S(1)}, u32[]{:S(2)}, u32[]{:S(2)}) collective-permute-start(bf16[24,3072]{1,0:T(8,128)(2,1)S(1)} %get-tuple-element.199), channel_id=1, source_target_pairs={{0,4},{1,5},{2,6},{3,7},{4,0},{5,1},{6,2},{7,3},{8,12},{9,13},{10,... | collective-permute-start | bytes 442376 | tf_op jit(solution)/shard_map/ppermute | solution.py:646
  292.8 10.3 %collective-permute-start.39 = (bf16[24,3072]{1,0:T(8,128)(2,1)S(1)}, bf16[24,3072]{1,0:T(8,128)(2,1)S(1)}, u32[]{:S(2)}, u32[]{:S(2)}) collective-permute-start(bf16[24,3072]{1,0:T(8,128)(2,1)S(1)} %get-tuple-element.200), channel_id=1, source_target_pairs={{0,6},{1,7},{2,0},{3,1},{4,2},{5,3},{6,4},{7,5},{8,14},{9,15},{10,... | collective-permute-start | bytes 442376 | tf_op jit(solution)/shard_map/ppermute | solution.py:646
  305.0 68.8 %collective-permute-start.60 = (bf16[24,3072]{1,0:T(8,128)(2,1)}, bf16[24,3072]{1,0:T(8,128)(2,1)}, u32[]{:S(2)}, u32[]{:S(2)}) collective-permute-start(bf16[24,3072]{1,0:T(8,128)(2,1)} %add_convert_fusion.10), channel_id=1, source_target_pairs={{0,8},{8,0},{16,24},{24,16},{1,9},{9,1},{17,25},{25,17},{2,10},{10... | collective-permute-start | bytes 442376 | tf_op jit(solution)/shard_map/ppermute | solution.py:634
  305.5 68.9 %collective-permute-start.61 = (bf16[24,3072]{1,0:T(8,128)(2,1)}, bf16[24,3072]{1,0:T(8,128)(2,1)}, u32[]{:S(2)}, u32[]{:S(2)}) collective-permute-start(bf16[24,3072]{1,0:T(8,128)(2,1)} %add_convert_fusion.10), channel_id=1, source_target_pairs={{0,16},{8,24},{16,0},{24,8},{1,17},{9,25},{17,1},{25,9},{2,18},{10... | collective-permute-start | bytes 442376 | tf_op jit(solution)/shard_map/ppermute | solution.py:634
  335.0 9.7 %collective-permute-start.44 = (bf16[4,24,1152]{2,1,0:T(8,128)(2,1)}, bf16[4,24,1152]{2,1,0:T(8,128)(2,1)}, u32[]{:S(2)}, u32[]{:S(2)}) collective-permute-start(bf16[4,24,1152]{2,1,0:T(8,128)(2,1)} %get-tuple-element.215), channel_id=1, source_target_pairs={{0,24},{8,16},{16,8},{24,0},{1,25},{9,17},{17,9},{25,1},{2,26},{10... | collective-permute-start | bytes 663560 | tf_op jit(solution)/shard_map/ppermute | solution.py:634
  336.0 11.9 %collective-permute-start.43 = (bf16[4,24,1152]{2,1,0:T(8,128)(2,1)}, bf16[4,24,1152]{2,1,0:T(8,128)(2,1)}, u32[]{:S(2)}, u32[]{:S(2)}) collective-permute-start(bf16[4,24,1152]{2,1,0:T(8,128)(2,1)} %get-tuple-element.214), channel_id=1, source_target_pairs={{0,16},{8,24},{16,0},{24,8},{1,17},{9,25},{17,1},{25,9},{2,18},{10... | collective-permute-start | bytes 663560 | tf_op jit(solution)/shard_map/ppermute | solution.py:634
  338.1 9.9 %collective-permute-start.42 = (bf16[4,24,1152]{2,1,0:T(8,128)(2,1)}, bf16[4,24,1152]{2,1,0:T(8,128)(2,1)}, u32[]{:S(2)}, u32[]{:S(2)}) collective-permute-start(bf16[4,24,1152]{2,1,0:T(8,128)(2,1)} %get-tuple-element.213), channel_id=1, source_target_pairs={{0,8},{8,0},{16,24},{24,16},{1,9},{9,1},{17,25},{25,17},{2,10},{10... | collective-permute-start | bytes 663560 | tf_op jit(solution)/shard_map/ppermute | solution.py:634
  365.2 9.2 %collective-permute-start.62 = (bf16[24,3072]{1,0:T(8,128)(2,1)}, bf16[24,3072]{1,0:T(8,128)(2,1)}, u32[]{:S(2)}, u32[]{:S(2)}) collective-permute-start(bf16[24,3072]{1,0:T(8,128)(2,1)} %add_convert_fusion.10), channel_id=1, source_target_pairs={{0,24},{8,16},{16,8},{24,0},{1,25},{9,17},{17,9},{25,1},{2,26},{10... | collective-permute-start | bytes 442376 | tf_op jit(solution)/shard_map/ppermute | solution.py:634
  370.9 19.8 %collective-permute-start.53 = (bf16[4,24,1152]{2,1,0:T(8,128)(2,1)}, bf16[4,24,1152]{2,1,0:T(8,128)(2,1)}, u32[]{:S(2)}, u32[]{:S(2)}) collective-permute-start(bf16[4,24,1152]{2,1,0:T(8,128)(2,1)} %get-tuple-element.219), channel_id=1, source_target_pairs={{0,24},{8,16},{16,8},{24,0},{1,25},{9,17},{17,9},{25,1},{2,26},{10... | collective-permute-start | bytes 663560 | tf_op jit(solution)/shard_map/ppermute | solution.py:634
  373.6 17.2 %collective-permute-start.52 = (bf16[4,24,1152]{2,1,0:T(8,128)(2,1)}, bf16[4,24,1152]{2,1,0:T(8,128)(2,1)}, u32[]{:S(2)}, u32[]{:S(2)}) collective-permute-start(bf16[4,24,1152]{2,1,0:T(8,128)(2,1)} %get-tuple-element.218), channel_id=1, source_target_pairs={{0,16},{8,24},{16,0},{24,8},{1,17},{9,25},{17,1},{25,9},{2,18},{10... | collective-permute-start | bytes 663560 | tf_op jit(solution)/shard_map/ppermute | solution.py:634
  373.7 17.0 %collective-permute-start.51 = (bf16[4,24,1152]{2,1,0:T(8,128)(2,1)}, bf16[4,24,1152]{2,1,0:T(8,128)(2,1)}, u32[]{:S(2)}, u32[]{:S(2)}) collective-permute-start(bf16[4,24,1152]{2,1,0:T(8,128)(2,1)} %get-tuple-element.217), channel_id=1, source_target_pairs={{0,8},{8,0},{16,24},{24,16},{1,9},{9,1},{17,25},{25,17},{2,10},{10... | collective-permute-start | bytes 663560 | tf_op jit(solution)/shard_map/ppermute | solution.py:634
  374.4 22.5 %collective-permute-start.63 = (bf16[96,768]{1,0:T(8,128)(2,1)}, bf16[96,768]{1,0:T(8,128)(2,1)S(1)}, u32[]{:S(2)}, u32[]{:S(2)}) collective-permute-start(bf16[96,768]{1,0:T(8,128)(2,1)} %reduce-scatter.2.cloned.1.call-done), channel_id=1, source_target_pairs={{0,8},{8,0},{16,24},{24,16},{1,9},{9,1},{17,25},{25,17},{2,10},{10... | collective-permute-start | bytes 442376 | tf_op jit(solution)/shard_map/ppermute | solution.py:634
  (93 other events, 1008.8 us)
Sparse Core Ops, SparseCore 0:
  10.2 26.6 all-gather.2
  39.1 63.7 all-gather.4
  251.8 32.2 reduce-scatter.1
